TPU v7x, 256 devices: a whole 4x4x8 slice. The times are simulated.
256 devices in a mesh: seq: 64 (over z, y, x_lo), head: 4 (over x_hi, core).
Axes of the slice: x: 4 (x_hi: 2, x_lo: 2; x = x_hi * 2 + x_lo), y: 4, z: 8, core: 2. Of those that a mesh axis runs over, the one named last changes fastest.
Arguments:
- queries: float32 [8192, 8192], P('seq', 'head'), may hold values from -48 to 48
- prefix_keys: float32 [40960, 512], P('seq', 'head'), may hold values from -5 to 5
- prefix_value_rows: float32 [40960, 512], P('seq', 'head'), may hold values from -6 to 6
- response_keys: float32 [8192, 512], P('seq', 'head'), may hold values from -6 to 6
- response_values: float32 [8192, 512], P('seq', 'head'), may hold values from -6 to 6
- out_grad: float32 [8192, 8192], P('seq', 'head'), may hold values from -6 to 6
- lengths: int32 [64], P('seq'), may hold values from 32 to 128
Outputs:
- grad_queries: float32 [8192, 8192], P(('seq', 'head'))
- grad_prefix_keys: float32 [40960, 512], P('seq', 'head')
- grad_prefix_values: float32 [40960, 512], P('seq', 'head')
- grad_resp_keys: float32 [8192, 512], P('seq', 'head')
- grad_resp_values: float32 [8192, 512], P('seq', 'head')
All inputs are finite; a program needn't handle non-finite values.
Results may differ from a plain program's by a relative error of at most 0.0003.
Values sent between devices are 32-bit elements; how exact they have to be, the bound alone decides.
No kernel may reach another device: no remote copies, remote signals or barrier semaphores. Data moves between devices by JAX's collectives and lax.ppermute only.
A program may use at most 128 MiB of HBM per device.

v0:
```python
import jax
import jax.numpy as jnp
from jax import lax
from jax.experimental import pallas as pl
from jax.experimental.pallas import tpu as pltpu
from jax.sharding import PartitionSpec as P

HEAD_SIZE = 128
WINDOW = 3
LOG2E = 1.4426950408889634
F32, BF16 = jnp.float32, jnp.bfloat16
PAIR = 2


def passed_along(block, axis, distance):
    devices = range(lax.axis_size(axis))
    route = [((i - distance) % len(devices), i) for i in devices]
    return lax.ppermute(block, axis, route)


def parts_of(x):
    high = x.astype(BF16)
    return high, (x - high.astype(F32)).astype(BF16)


def nt(a, b):
    return lax.dot_general(a, b, (((1,), (1,)), ((), ())), preferred_element_type=F32)


def nn(a, b):
    return lax.dot_general(a, b, (((1,), (0,)), ((), ())), preferred_element_type=F32)


def attention_kernel(length_ref, q_ref, g_ref, *refs):
    nb = WINDOW + 1
    keys, values = refs[:nb], refs[nb : 2 * nb]
    dq_ref = refs[2 * nb]
    dk_refs, dv_refs = refs[2 * nb + 1 : 3 * nb + 1], refs[3 * nb + 1 : 4 * nb + 1]
    ka, va, kt, dk_sum, dv_sum = refs[4 * nb + 1 :]
    step = pl.program_id(0)
    rows = q_ref.shape[0]
    total = ka.shape[0]
    sizes = [k.shape[0] for k in keys]
    factor = HEAD_SIZE**-0.5

    @pl.when(step == 0)
    def _():
        at = 0
        for k_ref, v_ref, size in zip(keys, values, sizes):
            high, low = parts_of(k_ref[...])
            ka[at : at + size, :] = jnp.concatenate([high, low, high], axis=1)
            kt[:, at : at + size] = jnp.concatenate(
                [high.astype(F32).T, low.astype(F32).T], axis=0
            ).astype(BF16)
            high, low = parts_of(v_ref[...])
            va[at : at + size, :] = jnp.concatenate([high, low, high], axis=1)
            at += size
        dk_sum[...] = jnp.zeros_like(dk_sum)
        dv_sum[...] = jnp.zeros_like(dv_sum)

    length = length_ref[0]

    def stacked(ref):
        return jnp.concatenate(
            [ref[:, j * HEAD_SIZE : (j + 1) * HEAD_SIZE] for j in range(PAIR)], axis=0
        )

    q = stacked(q_ref) * (factor * LOG2E)
    token = lax.broadcasted_iota(jnp.int32, (PAIR, rows, HEAD_SIZE), 1).reshape(
        PAIR * rows, HEAD_SIZE
    )
    g = jnp.where(token < length, stacked(g_ref), 0.0)
    qh, ql = parts_of(q)
    gh, gl = parts_of(g)
    scores = nt(ka[...], jnp.concatenate([qh, qh, ql], axis=1))
    dprobs = nt(va[...], jnp.concatenate([gh, gh, gl], axis=1))
    slot = lax.broadcasted_iota(jnp.int32, (sizes[-1], PAIR * rows), 0)
    query = lax.broadcasted_iota(jnp.int32, (sizes[-1], PAIR * rows), 1) % rows
    visible = (slot <= query) & (slot < length)
    cut = total - sizes[-1]
    scores = jnp.concatenate(
        [scores[:cut], jnp.where(visible, scores[cut:], -1e30)], axis=0
    )
    top = jnp.max(scores, axis=0, keepdims=True)
    e = jnp.exp2(scores - top)
    inverse = 1.0 / jnp.sum(e, axis=0, keepdims=True)
    dsum = jnp.sum(e * dprobs, axis=0, keepdims=True) * inverse
    probs = e * inverse
    ds = probs * (dprobs - dsum)
    ph, plow = parts_of(probs)
    sh, sl = parts_of(ds)
    gg = jnp.concatenate([gh, gl], axis=1)
    qq = jnp.concatenate([qh, ql], axis=1)
    dv_sum[...] += nn(ph, gg) + nn(plow, gg)
    dk_sum[...] += nn(sh, qq) + nn(sl, qq)
    both = nn(kt[...], sh)
    dq_t = (both[:HEAD_SIZE] + both[HEAD_SIZE:] + nn(kt[:HEAD_SIZE], sl)) * factor
    dq = dq_t.T
    for j in range(PAIR):
        dq_ref[:, j * HEAD_SIZE : (j + 1) * HEAD_SIZE] = dq[j * rows : (j + 1) * rows]

    @pl.when(step == pl.num_programs(0) - 1)
    def _():
        at = 0
        for dk_ref, dv_ref, size in zip(dk_refs, dv_refs, sizes):
            here = slice(at, at + size)
            dk_ref[...] = (dk_sum[here, :HEAD_SIZE] + dk_sum[here, HEAD_SIZE:]) * (1.0 / LOG2E)
            dv_ref[...] = dv_sum[here, :HEAD_SIZE] + dv_sum[here, HEAD_SIZE:]
            at += size


def attention_grads(lengths, queries, out_grad, keys, values):
    rows, width = queries.shape
    total = sum(k.shape[0] for k in keys)
    chunk = PAIR * HEAD_SIZE
    per_head = pl.BlockSpec((rows, chunk), lambda i: (0, i))
    whole = [pl.BlockSpec(k.shape, lambda i: (0, 0)) for k in keys]
    like = [jax.ShapeDtypeStruct(k.shape, F32) for k in keys]
    return pl.pallas_call(
        attention_kernel,
        grid=(width // chunk,),
        in_specs=[pl.BlockSpec(memory_space=pltpu.SMEM), per_head, per_head] + whole + whole,
        out_specs=[per_head] + whole + whole,
        out_shape=[jax.ShapeDtypeStruct((rows, width), F32)] + like + like,
        scratch_shapes=[
            pltpu.VMEM((total, 3 * HEAD_SIZE), BF16),
            pltpu.VMEM((total, 3 * HEAD_SIZE), BF16),
            pltpu.VMEM((2 * HEAD_SIZE, total), BF16),
            pltpu.VMEM((total, 2 * HEAD_SIZE), F32),
            pltpu.VMEM((total, 2 * HEAD_SIZE), F32),
        ],
        compiler_params=pltpu.CompilerParams(vmem_limit_bytes=56 * 2**20),
        cost_estimate=pl.CostEstimate(
            flops=2 * 15 * rows * width * total, bytes_accessed=8_000_000, transcendentals=0
        ),
        name="attention_grads",
    )(lengths, queries, out_grad, *keys, *values)


def per_device(
    queries, prefix_keys, prefix_value_rows, response_keys, response_values, out_grad, lengths
):
    keys, values = [prefix_keys], [prefix_value_rows]
    for offset in range(1, WINDOW):
        keys.append(passed_along(prefix_keys, "seq", -offset))
        values.append(passed_along(prefix_value_rows, "seq", -offset))
    keys.append(response_keys)
    values.append(response_values)
    grads = attention_grads(lengths, queries, out_grad, keys, values)
    grad_query, dk, dv = grads[0], grads[1 : WINDOW + 2], grads[WINDOW + 2 :]
    grad_k, grad_v = dk[0], dv[0]
    for offset in range(1, WINDOW):
        grad_k = grad_k + passed_along(dk[offset], "seq", offset)
        grad_v = grad_v + passed_along(dv[offset], "seq", offset)
    grad_queries = lax.all_to_all(grad_query, "head", split_axis=0, concat_axis=1, tiled=True)
    return (grad_queries, grad_k, grad_v, dk[WINDOW], dv[WINDOW])


def solution(mesh):
    placed = (P("seq", "head"),) * 6 + (P("seq"),)
    return jax.shard_map(
        per_device,
        mesh=mesh,
        in_specs=placed,
        out_specs=(P(("seq", "head"), None),) + (P("seq", "head"),) * 4,
        check_vma=False,
    )
```

profile of v0, /device:TPU:2, one launch (start us, length us, event | category | flops | bytes accessed | tf_op | source)
XLA Modules:
  0.0 117.4 jit_solution(1451656978890019074)
XLA Ops:
  0.6 2.3 %collective-permute-start = (f32[640,128]{1,0:T(8,128)}, f32[640,128]{1,0:T(8,128)S(1)}, u32[]{:S(2)}, u32[]{:S(2)}) collective-permute-start(f32[640,128]{1,0:T(8,128)} %refs_0_.1), channel_id=1, source_target_pairs={{4,0},{8,4},{12,8},{16,12},{20,16},{24,20},{28,24},{32,28},{36,32}... | collective-permute-start | bytes 983048 | tf_op jit(solution)/shard_map/ppermute | solution.py:18
  3.0 6.6 %collective-permute-start.1 = (f32[640,128]{1,0:T(8,128)}, f32[640,128]{1,0:T(8,128)S(1)}, u32[]{:S(2)}, u32[]{:S(2)}) collective-permute-start(f32[640,128]{1,0:T(8,128)} %refs_0_.1), channel_id=1, source_target_pairs={{8,0},{12,4},{16,8},{20,12},{24,16},{28,20},{32,24},{36,28},{40,32... | collective-permute-start | bytes 983048 | tf_op jit(solution)/shard_map/ppermute | solution.py:18
  9.6 1.7 %collective-permute-start.2 = (f32[640,128]{1,0:T(8,128)}, f32[640,128]{1,0:T(8,128)S(1)}, u32[]{:S(2)}, u32[]{:S(2)}) collective-permute-start(f32[640,128]{1,0:T(8,128)} %refs_4_.1), channel_id=1, source_target_pairs={{4,0},{8,4},{12,8},{16,12},{20,16},{24,20},{28,24},{32,28},{36,32}... | collective-permute-start | bytes 983048 | tf_op jit(solution)/shard_map/ppermute | solution.py:18
  11.2 0.5 collective-permute-start.3
  12.3 0.0 collective-permute-done.refs_1_
  12.3 0.0 copy-start.4
  12.3 13.1 %collective-permute-done.1.refs_2_ = f32[640,128]{1,0:T(8,128)S(1)} collective-permute-done((f32[640,128]{1,0:T(8,128)}, f32[640,128]{1,0:T(8,128)S(1)}, u32[]{:S(2)}, u32[]{:S(2)}) %collective-permute-start.1) | collective-permute-done | bytes 327712 | tf_op jit(solution)/shard_map/ppermute | solution.py:18
  25.5 0.0 copy-start.5
  25.5 0.0 collective-permute-done.2.refs_5_
  25.5 0.0 copy-start.6
  25.5 6.3 %collective-permute-done.3.refs_6_ = f32[640,128]{1,0:T(8,128)S(1)} collective-permute-done((f32[640,128]{1,0:T(8,128)}, f32[640,128]{1,0:T(8,128)S(1)}, u32[]{:S(2)}, u32[]{:S(2)}) %collective-permute-start.3) | collective-permute-done | bytes 327712 | tf_op jit(solution)/shard_map/ppermute | solution.py:18
  31.8 0.0 copy-done.4
  31.8 0.0 copy-done.5
  31.8 0.0 copy-done.6
  31.8 0.0 copy-start.7
  31.8 0.7 copy-done.7
  32.5 34.0 %attention_grads.1 = (f32[128,2048]{1,0:T(8,128)}, f32[640,128]{1,0:T(8,128)}, f32[640,128]{1,0:T(8,128)}, f32[640,128]{1,0:T(8,128)}, f32[128,128]{1,0:T(8,128)...) custom-call(s32[1]{0:T(128)S(6)} %copy.14.length_ref, ...), custom_call_target="tpu_custom_call" | custom-call | flops 16106127360 | bytes 8000000 | tf_op jit(solution)/shard_map/attention_grads/pallas_call | solution.py:119
  66.5 0.1 collective-permute-start.4
  66.6 1.6 %collective-permute-start.5 = (f32[640,128]{1,0:T(8,128)}, f32[640,128]{1,0:T(8,128)S(1)}, u32[]{:S(2)}, u32[]{:S(2)}) collective-permute-start(f32[640,128]{1,0:T(8,128)} %get-tuple-element.17), channel_id=1, source_target_pairs={{248,0},{252,4},{0,8},{4,12},{8,16},{12,20},{16,24},{20,28},{24,32... | collective-permute-start | bytes 983048 | tf_op jit(solution)/shard_map/ppermute | solution.py:18
  68.2 0.0 copy-start.3
  68.2 0.0 copy-start.2
  68.2 0.0 copy-start.1
  68.2 3.8 %all-to-all-start = ((f32[4,32,2048]{2,1,0:T(8,128)}), f32[4,32,2048]{2,1,0:T(8,128)S(1)}, u32[]{:S(2)}, u32[]{:S(2)}) async-start(f32[4,32,2048]{2,1,0:T(8,128)} %bitcast.5), calls=%async_computation | async-start | bytes 2097152 | tf_op jit(solution)/shard_map/all_to_all | solution.py:155
  72.0 0.0 copy-done.3
  72.0 3.6 %collective-permute-start.6 = (f32[640,128]{1,0:T(8,128)S(1)}, f32[640,128]{1,0:T(8,128)S(1)}, u32[]{:S(2)}, u32[]{:S(2)}) collective-permute-start(f32[640,128]{1,0:T(8,128)S(1)} %copy-done.3), channel_id=1, source_target_pairs={{252,0},{0,4},{4,8},{8,12},{12,16},{16,20},{20,24},{24,28},{28,32}... | collective-permute-start | bytes 983048 | tf_op jit(solution)/shard_map/ppermute | solution.py:18
  75.5 0.0 copy-done.2
  75.5 8.5 %collective-permute-start.7 = (f32[640,128]{1,0:T(8,128)S(1)}, f32[640,128]{1,0:T(8,128)S(1)}, u32[]{:S(2)}, u32[]{:S(2)}) collective-permute-start(f32[640,128]{1,0:T(8,128)S(1)} %copy-done.2), channel_id=1, source_target_pairs={{248,0},{252,4},{0,8},{4,12},{8,16},{12,20},{16,24},{20,28},{24,32... | collective-permute-start | bytes 983048 | tf_op jit(solution)/shard_map/ppermute | solution.py:18
  84.0 3.4 %collective-permute-done.4 = f32[640,128]{1,0:T(8,128)S(1)} collective-permute-done((f32[640,128]{1,0:T(8,128)}, f32[640,128]{1,0:T(8,128)S(1)}, u32[]{:S(2)}, u32[]{:S(2)}) %collective-permute-start.4) | collective-permute-done | bytes 327712 | tf_op jit(solution)/shard_map/ppermute | solution.py:18
  87.5 14.6 %collective-permute-done.5 = f32[640,128]{1,0:T(8,128)S(1)} collective-permute-done((f32[640,128]{1,0:T(8,128)}, f32[640,128]{1,0:T(8,128)S(1)}, u32[]{:S(2)}, u32[]{:S(2)}) %collective-permute-start.5) | collective-permute-done | bytes 327712 | tf_op jit(solution)/shard_map/ppermute | solution.py:18
  102.1 0.0 copy-done.1
  102.1 0.0 copy-start
  102.1 0.8 add_add_fusion.1
  102.8 1.7 %collective-permute-done.6 = f32[640,128]{1,0:T(8,128)S(1)} collective-permute-done((f32[640,128]{1,0:T(8,128)S(1)}, f32[640,128]{1,0:T(8,128)S(1)}, u32[]{:S(2)}, u32[]{:S(2)}) %collective-permute-start.6) | collective-permute-done | bytes 327712 | tf_op jit(solution)/shard_map/ppermute | solution.py:18
  104.6 11.0 %collective-permute-done.7 = f32[640,128]{1,0:T(8,128)S(1)} collective-permute-done((f32[640,128]{1,0:T(8,128)S(1)}, f32[640,128]{1,0:T(8,128)S(1)}, u32[]{:S(2)}, u32[]{:S(2)}) %collective-permute-start.7) | collective-permute-done | bytes 327712 | tf_op jit(solution)/shard_map/ppermute | solution.py:18
  115.5 0.0 copy-done
  115.5 0.8 add_add_fusion
  116.3 0.0 all-to-all-done
  116.3 1.0 copy.13
Async XLA Ops:
  0.6 11.7 %collective-permute-start = (f32[640,128]{1,0:T(8,128)}, f32[640,128]{1,0:T(8,128)S(1)}, u32[]{:S(2)}, u32[]{:S(2)}) collective-permute-start(f32[640,128]{1,0:T(8,128)} %refs_0_.1), channel_id=1, source_target_pairs={{4,0},{8,4},{12,8},{16,12},{20,16},{24,20},{28,24},{32,28},{36,32}... | collective-permute-start | bytes 983048 | tf_op jit(solution)/shard_map/ppermute | solution.py:18
  3.0 22.5 %collective-permute-start.1 = (f32[640,128]{1,0:T(8,128)}, f32[640,128]{1,0:T(8,128)S(1)}, u32[]{:S(2)}, u32[]{:S(2)}) collective-permute-start(f32[640,128]{1,0:T(8,128)} %refs_0_.1), channel_id=1, source_target_pairs={{8,0},{12,4},{16,8},{20,12},{24,16},{28,20},{32,24},{36,28},{40,32... | collective-permute-start | bytes 983048 | tf_op jit(solution)/shard_map/ppermute | solution.py:18
  9.6 15.9 %collective-permute-start.2 = (f32[640,128]{1,0:T(8,128)}, f32[640,128]{1,0:T(8,128)S(1)}, u32[]{:S(2)}, u32[]{:S(2)}) collective-permute-start(f32[640,128]{1,0:T(8,128)} %refs_4_.1), channel_id=1, source_target_pairs={{4,0},{8,4},{12,8},{16,12},{20,16},{24,20},{28,24},{32,28},{36,32}... | collective-permute-start | bytes 983048 | tf_op jit(solution)/shard_map/ppermute | solution.py:18
  11.2 20.6 %collective-permute-start.3 = (f32[640,128]{1,0:T(8,128)}, f32[640,128]{1,0:T(8,128)S(1)}, u32[]{:S(2)}, u32[]{:S(2)}) collective-permute-start(f32[640,128]{1,0:T(8,128)} %refs_4_.1), channel_id=1, source_target_pairs={{8,0},{12,4},{16,8},{20,12},{24,16},{28,20},{32,24},{36,28},{40,32... | collective-permute-start | bytes 983048 | tf_op jit(solution)/shard_map/ppermute | solution.py:18
  12.3 19.5 %copy-start.4 = (f32[640,128]{1,0:T(8,128)}, f32[640,128]{1,0:T(8,128)S(1)}, u32[]{:S(2)}) copy-start(f32[640,128]{1,0:T(8,128)S(1)} %collective-permute-done.refs_1_) | copy-start | bytes 983044
  25.5 6.3 %copy-start.5 = (f32[640,128]{1,0:T(8,128)}, f32[640,128]{1,0:T(8,128)S(1)}, u32[]{:S(2)}) copy-start(f32[640,128]{1,0:T(8,128)S(1)} %collective-permute-done.1.refs_2_) | copy-start | bytes 983044
  25.5 6.3 %copy-start.6 = (f32[640,128]{1,0:T(8,128)}, f32[640,128]{1,0:T(8,128)S(1)}, u32[]{:S(2)}) copy-start(f32[640,128]{1,0:T(8,128)S(1)} %collective-permute-done.2.refs_5_) | copy-start | bytes 983044
  31.8 0.7 copy-start.7
  66.5 20.9 %collective-permute-start.4 = (f32[640,128]{1,0:T(8,128)}, f32[640,128]{1,0:T(8,128)S(1)}, u32[]{:S(2)}, u32[]{:S(2)}) collective-permute-start(f32[640,128]{1,0:T(8,128)} %get-tuple-element.16), channel_id=1, source_target_pairs={{252,0},{0,4},{4,8},{8,12},{12,16},{16,20},{20,24},{24,28},{28,32}... | collective-permute-start | bytes 983048 | tf_op jit(solution)/shard_map/ppermute | solution.py:18
  66.6 35.5 %collective-permute-start.5 = (f32[640,128]{1,0:T(8,128)}, f32[640,128]{1,0:T(8,128)S(1)}, u32[]{:S(2)}, u32[]{:S(2)}) collective-permute-start(f32[640,128]{1,0:T(8,128)} %get-tuple-element.17), channel_id=1, source_target_pairs={{248,0},{252,4},{0,8},{4,12},{8,16},{12,20},{16,24},{20,28},{24,32... | collective-permute-start | bytes 983048 | tf_op jit(solution)/shard_map/ppermute | solution.py:18
  68.2 3.8 %copy-start.3 = (f32[640,128]{1,0:T(8,128)S(1)}, f32[640,128]{1,0:T(8,128)}, u32[]{:S(2)}) copy-start(f32[640,128]{1,0:T(8,128)} %get-tuple-element.19) | copy-start | bytes 983044
  68.2 7.4 %copy-start.2 = (f32[640,128]{1,0:T(8,128)S(1)}, f32[640,128]{1,0:T(8,128)}, u32[]{:S(2)}) copy-start(f32[640,128]{1,0:T(8,128)} %get-tuple-element.20) | copy-start | bytes 983044
  68.2 33.9 %copy-start.1 = (f32[640,128]{1,0:T(8,128)S(1)}, f32[640,128]{1,0:T(8,128)}, u32[]{:S(2)}) copy-start(f32[640,128]{1,0:T(8,128)} %get-tuple-element.15) | copy-start | bytes 983044
  68.2 48.2 %all-to-all-start = ((f32[4,32,2048]{2,1,0:T(8,128)}), f32[4,32,2048]{2,1,0:T(8,128)S(1)}, u32[]{:S(2)}, u32[]{:S(2)}) async-start(f32[4,32,2048]{2,1,0:T(8,128)} %bitcast.5), calls=%async_computation | async-start | bytes 2097152 | tf_op jit(solution)/shard_map/all_to_all | solution.py:155
  72.0 32.6 %collective-permute-start.6 = (f32[640,128]{1,0:T(8,128)S(1)}, f32[640,128]{1,0:T(8,128)S(1)}, u32[]{:S(2)}, u32[]{:S(2)}) collective-permute-start(f32[640,128]{1,0:T(8,128)S(1)} %copy-done.3), channel_id=1, source_target_pairs={{252,0},{0,4},{4,8},{8,12},{12,16},{16,20},{20,24},{24,28},{28,32}... | collective-permute-start | bytes 983048 | tf_op jit(solution)/shard_map/ppermute | solution.py:18
  75.5 40.0 %collective-permute-start.7 = (f32[640,128]{1,0:T(8,128)S(1)}, f32[640,128]{1,0:T(8,128)S(1)}, u32[]{:S(2)}, u32[]{:S(2)}) collective-permute-start(f32[640,128]{1,0:T(8,128)S(1)} %copy-done.2), channel_id=1, source_target_pairs={{248,0},{252,4},{0,8},{4,12},{8,16},{12,20},{16,24},{20,28},{24,32... | collective-permute-start | bytes 983048 | tf_op jit(solution)/shard_map/ppermute | solution.py:18
  102.1 13.5 %copy-start = (f32[640,128]{1,0:T(8,128)S(1)}, f32[640,128]{1,0:T(8,128)}, u32[]{:S(2)}) copy-start(f32[640,128]{1,0:T(8,128)} %get-tuple-element.18) | copy-start | bytes 983044
where the time goes:
time: 118 us; the launch traced here: 117 us
  waiting for transfers between devices  50.2 us (43%)
  Pallas kernels  34 us (29%)
  starting transfers between devices  28.5 us (24%)
  local copies, waits for them, and re-layouts  1.79 us (2%)
  other arithmetic  1.55 us (1%)
  between operations  1.33 us (1%)
    ppermute x8, waiting for transfers between devices, passed_along(): return lax.ppermute(block, axis, route)  50.2 us
    pallas_call x1, Pallas kernels, attention_grads(): pl.pallas_call(attention_kernel, grid=(width // chunk,), in_specs=[pl.Blo...  34 us
    ppermute x8, starting transfers between devices, passed_along(): return lax.ppermute(block, axis, route)  24.7 us
    all_to_all x1, starting transfers between devices, per_device(): lax.all_to_all(grad_query, 'head', split_axis=0, concat_axis=1, tiled=True)  3.82 us
  transfers between devices with their start and end apart: 9, of which 6 were waited for; matrix products, arithmetic and copies ran while one was open for 1% of the time, Pallas kernels for 0%

commit v1 on v0

v1 whole, which is shorter than its diff:
```python
import functools

import jax
import jax.numpy as jnp
from jax import lax
from jax.experimental import pallas as pl
from jax.experimental.pallas import tpu as pltpu
from jax.sharding import PartitionSpec as P

SIZE = 128
LOG2E = 1.4426950408889634
FACTOR = SIZE**-0.5
COST_CUT = 1
F32, BF16 = jnp.float32, jnp.bfloat16


def parts_of(x):
    high = x.astype(BF16)
    return high, (x - high.astype(F32)).astype(BF16)


def nt(a, b):
    return lax.dot_general(a, b, (((1,), (1,)), ((), ())), preferred_element_type=F32)


def nn(a, b):
    return lax.dot_general(a, b, (((1,), (0,)), ((), ())), preferred_element_type=F32)


def head_columns(head):
    return slice(head * SIZE, (head + 1) * SIZE)


def stacked(ref, first_head, pair):
    return jnp.concatenate([ref[:, head_columns(first_head + j)] for j in range(pair)], axis=0)


def load_rows(length, q_ref, g_ref, sub, pair):
    rows = q_ref.shape[0]
    q = stacked(q_ref, sub * pair, pair) * (FACTOR * LOG2E)
    token = lax.broadcasted_iota(jnp.int32, (pair, rows, SIZE), 1).reshape(pair * rows, SIZE)
    g = jnp.where(token < length, stacked(g_ref, sub * pair, pair), 0.0)
    return parts_of(q), parts_of(g)


def chunks_of(q_ref, pair):
    width = pair * q_ref.shape[0]
    for sub in range(q_ref.shape[1] // (pair * SIZE)):
        yield sub, slice(sub * width, (sub + 1) * width)


def keep_parts(refs, store):
    at = 0
    for ref in refs:
        high, low = parts_of(ref[...])
        store[at : at + ref.shape[0], :] = jnp.concatenate([high, low, high], axis=1)
        at += ref.shape[0]


def keep_turned(refs, store):
    at = 0
    for ref in refs:
        turned = ref[...].T
        high, low = parts_of(turned)
        store[:, at : at + ref.shape[0]] = jnp.concatenate([high, low], axis=0)
        at += ref.shape[0]


def masked(scores, length, rows, masked_rows):
    cut = scores.shape[0] - masked_rows
    slot = lax.broadcasted_iota(jnp.int32, (masked_rows, scores.shape[1]), 0)
    query = lax.broadcasted_iota(jnp.int32, (masked_rows, scores.shape[1]), 1) % rows
    visible = (slot <= query) & (slot < length)
    return jnp.concatenate([scores[:cut], jnp.where(visible, scores[cut:], -1e30)], axis=0)


def stats_rows(*rows):
    return jnp.concatenate(rows + (jnp.zeros((8 - len(rows), rows[0].shape[1]), F32),), axis=0)


def scores_and_dprobs(ka, va, rows):
    (qh, ql), (gh, gl) = rows
    scores = nt(ka[...], jnp.concatenate([qh, qh, ql], axis=1))
    dprobs = nt(va[...], jnp.concatenate([gh, gh, gl], axis=1))
    return scores, dprobs


def first_kernel(pair, key_count, count, masked_rows, length_ref, q_ref, g_ref, *refs):
    keys, values = refs[:key_count], refs[key_count:count]
    e_ref, dp_ref, stats_ref, ka, va = refs[count:]

    @pl.when(pl.program_id(0) == 0)
    def _():
        keep_parts(keys, ka)
        keep_parts(values, va)

    for sub, here in chunks_of(q_ref, pair):
        rows = load_rows(length_ref[0], q_ref, g_ref, sub, pair)
        scores, dprobs = scores_and_dprobs(ka, va, rows)
        if masked_rows:
            scores = masked(scores, length_ref[0], q_ref.shape[0], masked_rows)
        top = jnp.max(scores, axis=0, keepdims=True)
        e = jnp.exp2(scores - top)
        e_ref[:, here] = e
        dp_ref[:, here] = dprobs
        total = jnp.sum(e, axis=0, keepdims=True)
        weighted = jnp.sum(e * dprobs, axis=0, keepdims=True)
        stats_ref[:, here] = stats_rows(top, total, weighted)


def add_products(probs, ds, rows, kt, dk_sum, dv_sum):
    (qh, ql), (gh, gl) = rows
    ph, plow = parts_of(probs)
    sh, sl = parts_of(ds)
    gg = jnp.concatenate([gh, gl], axis=1)
    qq = jnp.concatenate([qh, ql], axis=1)
    dv_sum[...] += nn(jnp.concatenate([ph, plow], axis=1), jnp.concatenate([gg, gg], axis=0))
    dk_sum[...] += nn(jnp.concatenate([sh, sl], axis=1), jnp.concatenate([qq, qq], axis=0))
    both = nn(kt[...], sh)
    return ((both[:SIZE] + both[SIZE:] + nn(kt[:SIZE], sl)) * FACTOR).T


def store_query_grad(dq, before_ref, dq_ref, sub, pair):
    rows = dq_ref.shape[0]
    for j in range(pair):
        here = head_columns(sub * pair + j)
        part = dq[j * rows : (j + 1) * rows]
        dq_ref[:, here] = part if before_ref is None else part + before_ref[:, here]


def store_sums(refs, before, kept, scale):
    at = 0
    for j, ref in enumerate(refs):
        here = slice(at, at + ref.shape[0])
        part = (kept[here, :SIZE] + kept[here, SIZE:]) * scale
        ref[...] = part + before[j][...] if before else part
        at += ref.shape[0]


def start_sums(dk_sum, dv_sum):
    dk_sum[...] = jnp.zeros_like(dk_sum)
    dv_sum[...] = jnp.zeros_like(dv_sum)


def middle_kernel(pair, value_count, length_ref, q_ref, g_ref, stats_a, stats_b, k_ref, *refs):
    values = refs[:value_count]
    dq_ref, final_ref, dk_ref, dv_ref, ka, va, kt, dk_sum, dv_sum = refs[value_count:]

    @pl.when(pl.program_id(0) == 0)
    def _():
        keep_parts([k_ref], ka)
        keep_parts(values, va)
        keep_turned([k_ref], kt)
        start_sums(dk_sum, dv_sum)

    for sub, here in chunks_of(q_ref, pair):
        rows = load_rows(length_ref[0], q_ref, g_ref, sub, pair)
        scores, dprobs = scores_and_dprobs(ka, va, rows)
        top_a, top_b = stats_a[0:1, here], stats_b[0:1, here]
        top = jnp.maximum(jnp.maximum(top_a, top_b), jnp.max(scores, axis=0, keepdims=True))
        e = jnp.exp2(scores - top)
        fade_a, fade_b = jnp.exp2(top_a - top), jnp.exp2(top_b - top)
        total = stats_a[1:2, here] * fade_a + stats_b[1:2, here] * fade_b
        total = total + jnp.sum(e, axis=0, keepdims=True)
        weighted = stats_a[2:3, here] * fade_a + stats_b[2:3, here] * fade_b
        weighted = weighted + jnp.sum(e * dprobs, axis=0, keepdims=True)
        inverse = 1.0 / total
        dsum = weighted * inverse
        final_ref[:, here] = stats_rows(fade_a * inverse, fade_b * inverse, dsum)
        probs = e * inverse
        ds = probs * (dprobs - dsum)
        dq = add_products(probs, ds, rows, kt, dk_sum, dv_sum)
        store_query_grad(dq, None, dq_ref, sub, pair)

    @pl.when(pl.program_id(0) == pl.num_programs(0) - 1)
    def _():
        store_sums([dk_ref], [], dk_sum, 1.0 / LOG2E)
        store_sums([dv_ref], [], dv_sum, 1.0)


def last_kernel(
    pair, count, before_count, scale_row, pieces,
    length_ref, place_ref, q_ref, g_ref, before_ref, e_ref, dp_ref, final_ref, *refs,
):
    keys, refs = refs[:count], refs[count:]
    before_dk, before_dv = refs[:before_count], refs[before_count : 2 * before_count]
    refs = refs[2 * before_count :]
    dq_refs, refs = refs[:pieces], refs[pieces:]
    dk_refs, dv_refs = refs[:count], refs[count : 2 * count]
    kt, dk_sum, dv_sum, *held = refs[2 * count :]
    dq_ref = held[0] if held else dq_refs[0]

    @pl.when(pl.program_id(0) == 0)
    def _():
        keep_turned(keys, kt)
        start_sums(dk_sum, dv_sum)

    for sub, here in chunks_of(q_ref, pair):
        rows = load_rows(length_ref[0], q_ref, g_ref, sub, pair)
        probs = e_ref[:, here] * final_ref[scale_row : scale_row + 1, here]
        ds = probs * (dp_ref[:, here] - final_ref[2:3, here])
        dq = add_products(probs, ds, rows, kt, dk_sum, dv_sum)
        store_query_grad(dq, before_ref, dq_ref, sub, pair)
    if held:
        size = dq_ref.shape[0] // pieces
        for j in range(pieces):
            at = pl.multiple_of((place_ref[0] ^ j) * size, size)
            dq_refs[j][...] = dq_ref[pl.ds(at, size), :]

    @pl.when(pl.program_id(0) == pl.num_programs(0) - 1)
    def _():
        store_sums(dk_refs, before_dk, dk_sum, 1.0 / LOG2E)
        store_sums(dv_refs, before_dv, dv_sum, 1.0)


SMEM = pl.BlockSpec(memory_space=pltpu.SMEM)


def shape_of(*dims):
    return jax.ShapeDtypeStruct(dims, F32)


def by_columns(rows, width, first=0):
    return pl.BlockSpec((rows, width), lambda i: (0, i + first))


def whole(arrays):
    return [pl.BlockSpec(a.shape, lambda i: (0, 0)) for a in arrays]


def like(arrays):
    return [shape_of(*a.shape) for a in arrays]


def settings(products, rows, width, total, moved):
    return dict(
        compiler_params=pltpu.CompilerParams(vmem_limit_bytes=24 * 2**20),
        cost_estimate=pl.CostEstimate(
            flops=2 * products * 4 * rows * width * total // COST_CUT,
            bytes_accessed=moved // COST_CUT,
            transcendentals=0,
        ),
    )


def first_pass(lengths, queries, out_grad, keys, values, masked_rows, name, pair=8, step=8):
    rows, width = queries.shape
    total = sum(k.shape[0] for k in keys)
    slots = rows * width // SIZE
    per_head, per_slot = by_columns(rows, step * SIZE), by_columns(total, step * rows)
    return pl.pallas_call(
        functools.partial(first_kernel, pair, len(keys), len(keys) + len(values), masked_rows),
        grid=(width // (step * SIZE),),
        in_specs=[SMEM, per_head, per_head] + whole(keys) + whole(values),
        out_specs=[per_slot, per_slot, by_columns(8, step * rows)],
        out_shape=[shape_of(total, slots)] * 2 + [shape_of(8, slots)],
        scratch_shapes=[pltpu.VMEM((total, 3 * SIZE), BF16)] * 2,
        name=name,
        **settings(2, rows, width, total, 8 * total * slots),
    )(lengths, queries, out_grad, *keys, *values)


def middle_pass(lengths, queries, out_grad, stats_a, stats_b, key_block, values, pair=8, step=16):
    rows, width = queries.shape
    total = key_block.shape[0]
    slots = rows * width // SIZE
    per_head, stats = by_columns(rows, step * SIZE), by_columns(8, step * rows)
    return pl.pallas_call(
        functools.partial(middle_kernel, pair, len(values)),
        grid=(width // (step * SIZE),),
        in_specs=[SMEM, per_head, per_head, stats, stats] + whole([key_block]) + whole(values),
        out_specs=[per_head, stats] + whole([key_block, key_block]),
        out_shape=[shape_of(rows, width), shape_of(8, slots)] + like([key_block, key_block]),
        scratch_shapes=[pltpu.VMEM((total, 3 * SIZE), BF16)] * 2
        + [pltpu.VMEM((2 * SIZE, total), BF16)]
        + [pltpu.VMEM((total, 2 * SIZE), F32)] * 2,
        name="middle_pass",
        **settings(5, rows, width, total, 5_000_000),
    )(lengths, queries, out_grad, stats_a, stats_b, key_block, *values)


def last_pass(
    lengths, queries, out_grad, place, before, e, dp, final, scale_row, keys, name,
    first=0, heads=16, before_sums=(), pieces=1, pair=4, step=4,
):
    rows = queries.shape[0]
    total = sum(k.shape[0] for k in keys)
    start = first // step
    per_head = by_columns(rows, step * SIZE, start)
    per_slot = by_columns(total, step * rows, start)
    stats = by_columns(8, step * rows, start)
    return pl.pallas_call(
        functools.partial(last_kernel, pair, len(keys), len(before_sums) // 2, scale_row, pieces),
        grid=(heads // step,),
        in_specs=[SMEM, SMEM, per_head, per_head, per_head, per_slot, per_slot, stats]
        + whole(keys) + whole(before_sums),
        out_specs=[by_columns(rows // pieces, step * SIZE)] * pieces + whole(keys) + whole(keys),
        out_shape=[shape_of(rows // pieces, heads * SIZE)] * pieces + like(keys) + like(keys),
        scratch_shapes=[pltpu.VMEM((2 * SIZE, total), BF16)]
        + [pltpu.VMEM((total, 2 * SIZE), F32)] * 2
        + [pltpu.VMEM((rows, step * SIZE), F32)] * (pieces > 1),
        name=name,
        **settings(3, rows, heads * SIZE, total, 8 * total * heads * rows),
    )(lengths, place, queries, out_grad, before, e, dp, final, *keys, *before_sums)


def sum_kernel(odd_ref, own_ref, near_ref, far_ref, out_ref):
    near = jnp.where(odd_ref[0] == 1, near_ref[...], 0.0)
    out_ref[...] = own_ref[...] + near + far_ref[...]


def gather_kernel(count, place_ref, *refs):
    out_ref, half = refs[-1], refs[0].shape[1]
    for j in range(count):
        for k in range(2):
            at = pl.multiple_of(((place_ref[0] ^ j) * 2 + k) * half, half)
            out_ref[:, pl.ds(at, half)] = refs[2 * j + k][...]


def sum_pass(odd, own, near, far, name):
    blocks = whole([own, near, far])
    return pl.pallas_call(
        sum_kernel,
        grid=(1,),
        in_specs=[SMEM] + blocks,
        out_specs=blocks[0],
        out_shape=shape_of(*own.shape),
        name=name,
    )(odd, own, near, far)


def gather_pass(place, parts):
    rows, half = parts[0].shape
    return pl.pallas_call(
        functools.partial(gather_kernel, len(parts) // 2),
        grid=(1,),
        in_specs=[SMEM] + whole(parts),
        out_specs=pl.BlockSpec((rows, len(parts) * half), lambda i: (0, 0)),
        out_shape=shape_of(rows, len(parts) * half),
        name="gather_queries",
    )(place, *parts)


def per_device(
    queries, prefix_keys, prefix_value_rows, response_keys, response_values, out_grad, lengths
):
    count = lax.axis_size("seq")
    head_devices = lax.axis_size("head")
    even = lax.axis_index("seq") % 2 == 0
    odd = (lax.axis_index("seq") % 2).astype(jnp.int32).reshape(1)
    place = lax.axis_index("head").astype(jnp.int32).reshape(1)
    rows, width = queries.shape
    heads = width // SIZE
    half = prefix_keys.shape[0] // 2

    def from_two_on(block):
        return lax.ppermute(block, "seq", [((i + 2) % count, i) for i in range(count)])

    def to_two_on(block):
        return lax.ppermute(block, "seq", [(i, (i + 2) % count) for i in range(count)])

    def swapped(block):
        return lax.ppermute(block, "seq", [(i, i ^ 1) for i in range(count)])

    def exchanged(block, bits):
        return lax.ppermute(block, "head", [(i, i ^ bits) for i in range(head_devices)])

    def split_grads(grads):
        return grads[:head_devices], grads[head_devices:]

    args = (lengths, queries, out_grad)
    value_parts = [prefix_value_rows[:half], prefix_value_rows[half:]]
    far_k = from_two_on(prefix_keys)
    far_v = [from_two_on(part) for part in value_parts]

    own_keys, own_values = [prefix_keys, response_keys], [prefix_value_rows, response_values]
    own_e, own_dp, own_stats = first_pass(*args, own_keys, own_values, rows, "own_scores")
    own_stats, far_k = lax.optimization_barrier((own_stats, far_k))
    near_k = swapped(jnp.where(even, far_k, prefix_keys))
    near_v = []
    for j in range(2):
        own_stats, far_v[j] = lax.optimization_barrier((own_stats, far_v[j]))
        chosen = jnp.where(even, far_v[j], value_parts[j])
        near_v.append(swapped(chosen))
    own_stats, far_k, chosen = lax.optimization_barrier((own_stats, far_k, chosen))
    far_e, far_dp, far_stats = first_pass(*args, [far_k], far_v, 0, "far_scores")
    near_dq, final, near_dk, near_dv = middle_pass(*args, own_stats, far_stats, near_k, near_v)

    from_near_dv, from_near_dk = swapped(near_dv), swapped(near_dk)
    far_dq, far_dk, far_dv = last_pass(
        *args, place, near_dq, far_e, far_dp, final, 1, [far_k], "far_grads"
    )
    to_far_dv = far_dv + jnp.where(even, from_near_dv, 0.0)
    from_far_dv = to_two_on(to_far_dv)
    far_dq, to_far_dv = lax.optimization_barrier((far_dq, to_far_dv))
    dq_a, sums = split_grads(last_pass(
        *args, place, far_dq, own_e, own_dp, final, 0, own_keys, "own_grads_a",
        first=0, heads=heads // 2, pieces=head_devices,
    ))
    got_a = [dq_a[0]] + [exchanged(dq_a[j], j) for j in range(1, head_devices)]
    to_far_dk = far_dk + jnp.where(even, from_near_dk, 0.0)
    sums, to_far_dk, far_dq = lax.optimization_barrier((sums, to_far_dk, far_dq))
    from_far_dk = to_two_on(to_far_dk)
    dq_b, (own_dk, resp_dk, own_dv, resp_dv) = split_grads(last_pass(
        *args, place, far_dq, own_e, own_dp, final, 0, own_keys, "own_grads_b",
        first=heads // 2, heads=heads // 2, before_sums=sums, pieces=head_devices,
    ))
    got_a, dq_b = lax.optimization_barrier((got_a, dq_b))
    got_b = [dq_b[0]] + [exchanged(dq_b[j], j) for j in range(1, head_devices)]
    grad_v = sum_pass(odd, own_dv, from_near_dv, from_far_dv, "sum_values")
    grad_k = sum_pass(odd, own_dk, from_near_dk, from_far_dk, "sum_keys")
    got_b, grad_k, grad_v = lax.optimization_barrier((got_b, grad_k, grad_v))
    grad_queries = gather_pass(place, [x for pair in zip(got_a, got_b) for x in pair])
    return (grad_queries, grad_k, grad_v, resp_dk, resp_dv)


def solution(mesh):
    placed = (P("seq", "head"),) * 6 + (P("seq"),)
    return jax.shard_map(
        per_device,
        mesh=mesh,
        in_specs=placed,
        out_specs=(P(("seq", "head"), None),) + (P("seq", "head"),) * 4,
        check_vma=False,
    )
```

time: 118 us -> 87.8 us (0.74)
  the two profiles are of different devices: /device:TPU:2 before, /device:TPU:1 now
where the time goes in v1:
time: 87.8 us; the launch traced here: 87.4 us
  Pallas kernels  38.2 us (44%)
  starting transfers between devices  29.5 us (34%)
  local copies, waits for them, and re-layouts  11.2 us (13%)
  waiting for transfers between devices  6.83 us (8%)
  between operations  1.5 us (2%)
    pallas_call x3, Pallas kernels, last_pass(): pl.pallas_call(functools.partial(last_kernel, pair, len(keys), len(before...  15 us
    ppermute x6, starting transfers between devices, exchanged(): lax.ppermute(block, 'head', [(i, i ^ bits) for i in range(head_devices)])  12 us
    ppermute x3, starting transfers between devices, from_two_on(): lax.ppermute(block, 'seq', [((i + 2) % count, i) for i in range(count)])  11.8 us
    unnamed x44, local copies, waits for them, and re-layouts  10.3 us
    pallas_call x2, Pallas kernels, first_pass(): pl.pallas_call(functools.partial(first_kernel, pair, len(keys), len(keys)...  9.22 us
    pallas_call x1, Pallas kernels, middle_pass(): pl.pallas_call(functools.partial(middle_kernel, pair, len(values)), grid=...  7.79 us
    ppermute x5, starting transfers between devices, swapped(): return lax.ppermute(block, 'seq', [(i, i ^ 1) for i in range(count)])  4.37 us
    pallas_call x2, Pallas kernels, sum_pass(): pl.pallas_call(sum_kernel, grid=(1,), in_specs=[SMEM] + blocks, out_specs...  3.88 us
  transfers between devices with their start and end apart: 16, of which 4 were waited for; matrix products, arithmetic and copies ran while one was open for 1% of the time, Pallas kernels for 32%

profile of v1, /device:TPU:1, one launch (start us, length us, event | category | flops | bytes accessed | tf_op | source)
XLA Modules:
  0.0 87.4 jit_solution(10730851390155235601)
XLA Ops:
  0.6 8.9 %collective-permute-start = (f32[640,128]{1,0:T(8,128)}, f32[640,128]{1,0:T(8,128)S(1)}, u32[]{:S(2)}, u32[]{:S(2)}) collective-permute-start(f32[640,128]{1,0:T(8,128)} %refs_0_.5), channel_id=1, source_target_pairs={{8,0},{12,4},{16,8},{20,12},{24,16},{28,20},{32,24},{36,28},{40,32... | collective-permute-start | bytes 983048 | tf_op jit(solution)/shard_map/ppermute | solution.py:357
  9.6 0.9 %slice.6 = f32[320,128]{1,0:T(8,128)S(1)} slice(f32[640,128]{1,0:T(8,128)} %refs_2_.1), slice={[0:320], [0:128]} | slice | bytes 327680 | tf_op jit(solution)/shard_map/slice | solution.py:372
  10.5 0.5 collective-permute-start.1
  11.7 0.0 copy-start
  11.7 1.2 %copy-done = f32[128,2048]{1,0:T(8,128)S(1)} copy-done((f32[128,2048]{1,0:T(8,128)S(1)}, f32[128,2048]{1,0:T(8,128)}, u32[]{:S(2)}) %copy-start) | copy-done | bytes 1048600
  12.9 1.2 %copy-done.1 = f32[128,2048]{1,0:T(8,128)S(1)} copy-done((f32[128,2048]{1,0:T(8,128)S(1)}, f32[128,2048]{1,0:T(8,128)}, u32[]{:S(2)}) %copy-start.1) | copy-done | bytes 1048600
  14.1 1.0 %copy-done.2 = f32[640,128]{1,0:T(8,128)S(1)} copy-done((f32[640,128]{1,0:T(8,128)S(1)}, f32[640,128]{1,0:T(8,128)}, u32[]{:S(2)}) %copy-start.2) | copy-done | bytes 327704
  15.1 1.0 %copy-done.4 = f32[640,128]{1,0:T(8,128)S(1)} copy-done((f32[640,128]{1,0:T(8,128)S(1)}, f32[640,128]{1,0:T(8,128)}, u32[]{:S(2)}) %copy-start.4) | copy-done | bytes 327704
  16.1 0.8 copy-done.7
  16.9 0.8 copy-done.11
  17.8 5.0 %own_scores.1 = (f32[768,2048]{1,0:T(8,128)S(1)}, f32[768,2048]{1,0:T(8,128)S(1)}, f32[8,2048]{1,0:T(8,128)S(1)}) custom-call(s32[1]{0:T(128)S(6)} %copy.12.length_ref, f32[128,2048]{1,0:T(8,128)S(1)} %copy-done, f32[128,2048]{1,0:T(8,128)S(1)} %copy-done.1, f32[640,128]{1,0:T(8,128)S(1)} %copy-done.2, f32[128,128]{1,0:T(8,128)S(1)} %copy-done.7, ...), custom_call_target="tpu_custom_call" | custom-call | flops 3221225472 | bytes 12582912 | tf_op jit(solution)/shard_map/own_scores/pallas_call | solution.py:251
  22.8 0.0 collective-permute-done.refs_0_
  22.8 0.0 collective-permute-done.1.refs_1_
  22.9 1.3 %collective-permute-start.4 = (f32[320,128]{1,0:T(8,128)S(1)}, f32[320,128]{1,0:T(8,128)S(1)}, u32[]{:S(2)}, u32[]{:S(2)}) collective-permute-start(f32[320,128]{1,0:T(8,128)S(1)} %get-tuple-element.121), channel_id=1, source_target_pairs={{0,4},{4,0},{8,12},{12,8},{16,20},{20,16},{24,28},{28,24},{32,36},... | collective-permute-start | bytes 491528 | tf_op jit(solution)/shard_map/ppermute | solution.py:363
  24.2 2.4 %collective-permute-start.2 = (f32[320,128]{1,0:T(8,128)S(1)}, f32[320,128]{1,0:T(8,128)S(1)}, u32[]{:S(2)}, u32[]{:S(2)}) collective-permute-start(f32[320,128]{1,0:T(8,128)S(1)} %get-tuple-element.122), channel_id=1, source_target_pairs={{8,0},{12,4},{16,8},{20,12},{24,16},{28,20},{32,24},{36,28},{40,32... | collective-permute-start | bytes 491528 | tf_op jit(solution)/shard_map/ppermute | solution.py:357
  26.6 0.3 collective-permute-start.3
  26.9 1.9 %collective-permute-done.2.refs_2_ = f32[320,128]{1,0:T(8,128)S(1)} collective-permute-done((f32[320,128]{1,0:T(8,128)S(1)}, f32[320,128]{1,0:T(8,128)S(1)}, u32[]{:S(2)}, u32[]{:S(2)}) %collective-permute-start.2) | collective-permute-done | bytes 163872 | tf_op jit(solution)/shard_map/ppermute | solution.py:357
  28.8 0.5 collective-permute-start.5
  29.3 4.2 %far_scores.1 = (f32[640,2048]{1,0:T(8,128)S(1)}, f32[640,2048]{1,0:T(8,128)S(1)}, f32[8,2048]{1,0:T(8,128)S(1)}) custom-call(s32[1]{0:T(128)S(6)} %copy.12.length_ref, f32[128,2048]{1,0:T(8,128)S(1)} %copy-done, f32[128,2048]{1,0:T(8,128)S(1)} %copy-done.1, f32[640,128]{1,0:T(8,128)S(1)} %collective-permute-done.refs_0_, ...), custom_call_target="tpu_custom_call" | custom-call | flops 2684354560 | bytes 10485760 | tf_op jit(solution)/shard_map/far_scores/pallas_call | solution.py:251
  33.5 0.0 collective-permute-done.4.refs_0_
  33.5 3.7 %collective-permute-done.5.refs_1_ = f32[320,128]{1,0:T(8,128)S(1)} collective-permute-done((f32[320,128]{1,0:T(8,128)S(1)}, f32[320,128]{1,0:T(8,128)S(1)}, u32[]{:S(2)}, u32[]{:S(2)}) %collective-permute-start.5) | collective-permute-done | bytes 163872 | tf_op jit(solution)/shard_map/ppermute | solution.py:363
  37.2 0.0 collective-permute-done.3.k_ref
  37.3 7.8 %middle_pass.1 = (f32[128,2048]{1,0:T(8,128)S(1)}, f32[8,2048]{1,0:T(8,128)S(1)}, f32[640,128]{1,0:T(8,128)S(1)}, f32[640,128]{1,0:T(8,128)S(1)}) custom-call(s32[1]{0:T(128)S(6)} %copy.12.length_ref, f32[128,2048]{1,0:T(8,128)S(1)} %copy-done, f32[128,2048]{1,0:T(8,128)S(1)} %copy-done.1, f32[8,2048]{1,0:T(8,128)S(1)} %get-tuple-element.69.stats_a, ...), custom_call_target="tpu_custom_call" | custom-call | flops 6710886400 | bytes 5000000 | tf_op jit(solution)/shard_map/middle_pass/pallas_call | solution.py:268
  45.0 1.9 %collective-permute-start.6 = (f32[640,128]{1,0:T(8,128)S(1)}, f32[640,128]{1,0:T(8,128)S(1)}, u32[]{:S(2)}, u32[]{:S(2)}) collective-permute-start(f32[640,128]{1,0:T(8,128)S(1)} %get-tuple-element.79), channel_id=1, source_target_pairs={{0,4},{4,0},{8,12},{12,8},{16,20},{20,16},{24,28},{28,24},{32,36},... | collective-permute-start | bytes 983048 | tf_op jit(solution)/shard_map/ppermute | solution.py:363
  46.9 0.3 collective-permute-start.10
  47.3 6.5 %far_grads.1 = (f32[128,2048]{1,0:T(8,128)S(1)}, f32[640,128]{1,0:T(8,128)S(1)}, f32[640,128]{1,0:T(8,128)S(1)}) custom-call(s32[1]{0:T(128)S(6)} %copy.12.length_ref, s32[1]{0:T(128)} %bitcast.place_ref, f32[128,2048]{1,0:T(8,128)S(1)} %copy-done, f32[128,2048]{1,0:T(8,128)S(1)} %copy-done.1, f32[128,2048]{1,0:T(8,128)S(1)} %get-tuple-element.73.before_ref, ...), custom_call_target="tpu_custom_call" | custom-call | flops 4026531840 | bytes 10485760 | tf_op jit(solution)/shard_map/far_grads/pallas_call | solution.py:292
  53.7 0.0 collective-permute-done.6.near_ref
  53.8 0.0 copy-start.13
  53.8 0.1 select_add_fusion.1
  53.8 1.2 %collective-permute-start.15 = (f32[640,128]{1,0:T(8,128)S(1)}, f32[640,128]{1,0:T(8,128)S(1)}, u32[]{:S(2)}, u32[]{:S(2)}) collective-permute-start(f32[640,128]{1,0:T(8,128)S(1)} %select_add_fusion.1), channel_id=1, source_target_pairs={{0,8},{4,12},{8,16},{12,20},{16,24},{20,28},{24,32},{28,36},{32,40... | collective-permute-start | bytes 983048 | tf_op jit(solution)/shard_map/ppermute | solution.py:360
  55.0 0.0 copy-done.3
  55.0 0.0 copy-done.8
  55.0 3.9 %own_grads_a.1 = (f32[32,1024]{1,0:T(8,128)S(1)}, f32[32,1024]{1,0:T(8,128)S(1)}, f32[32,1024]{1,0:T(8,128)S(1)}, f32[32,1024]{1,0:T(8,128)S(1)}, f32[640,128]{1...) custom-call(s32[1]{0:T(128)S(6)} %copy.12.length_ref, s32[1]{0:T(128)} %bitcast.place_ref, ...), custom_call_target="tpu_custom_call" | custom-call | flops 2415919104 | bytes 6291456 | tf_op jit(solution)/shard_map/own_grads_a/pallas_call | solution.py:292
  58.9 0.0 copy-done.13
  58.9 0.0 copy-start.9
  58.9 0.1 collective-permute-done.10.near_ref
  59.1 5.0 %collective-permute-start.7 = (f32[32,1024]{1,0:T(8,128)S(1)}, f32[32,1024]{1,0:T(8,128)S(1)}, u32[]{:S(2)}, u32[]{:S(2)}) collective-permute-start(f32[32,1024]{1,0:T(8,128)S(1)} %get-tuple-element.84), channel_id=1, source_target_pairs={{0,1},{1,0},{2,3},{3,2},{4,5},{5,4},{6,7},{7,6},{8,9},{9,8},{10,11... | collective-permute-start | bytes 393224 | tf_op jit(solution)/shard_map/ppermute | solution.py:366
  64.1 2.8 %collective-permute-start.8 = (f32[32,1024]{1,0:T(8,128)S(1)}, f32[32,1024]{1,0:T(8,128)S(1)}, u32[]{:S(2)}, u32[]{:S(2)}) collective-permute-start(f32[32,1024]{1,0:T(8,128)S(1)} %get-tuple-element.85), channel_id=1, source_target_pairs={{0,2},{1,3},{2,0},{3,1},{4,6},{5,7},{6,4},{7,5},{8,10},{9,11},{10,... | collective-permute-start | bytes 393224 | tf_op jit(solution)/shard_map/ppermute | solution.py:366
  66.9 0.5 collective-permute-start.9
  67.3 0.1 collective-permute-start.14
  67.4 4.6 %own_grads_b.1 = (f32[32,1024]{1,0:T(8,128)S(1)}, f32[32,1024]{1,0:T(8,128)S(1)}, f32[32,1024]{1,0:T(8,128)S(1)}, f32[32,1024]{1,0:T(8,128)S(1)}, f32[640,128]{1...) custom-call(s32[1]{0:T(128)S(6)} %copy.12.length_ref, s32[1]{0:T(128)} %bitcast.place_ref, ...), custom_call_target="tpu_custom_call" | custom-call | flops 2415919104 | bytes 6291456 | tf_op jit(solution)/shard_map/own_grads_b/pallas_call | solution.py:292
  72.0 0.7 copy-done.5
  72.7 0.7 copy-done.6
  73.5 0.6 copy-done.10
  74.1 0.0 collective-permute-done.7.refs_2_
  74.1 0.0 collective-permute-done.8.refs_4_
  74.1 0.0 collective-permute-done.9.refs_6_
  74.1 0.5 collective-permute-start.11
  74.7 2.7 %collective-permute-start.12 = (f32[32,1024]{1,0:T(8,128)S(1)}, f32[32,1024]{1,0:T(8,128)S(1)}, u32[]{:S(2)}, u32[]{:S(2)}) collective-permute-start(f32[32,1024]{1,0:T(8,128)S(1)} %get-tuple-element.105), channel_id=1, source_target_pairs={{0,2},{1,3},{2,0},{3,1},{4,6},{5,7},{6,4},{7,5},{8,10},{9,11},{10,... | collective-permute-start | bytes 393224 | tf_op jit(solution)/shard_map/ppermute | solution.py:366
  77.4 0.5 collective-permute-start.13
  77.9 0.0 collective-permute-done.15.far_ref
  77.9 0.7 copy-done.14
  78.6 1.9 %sum_values.1 = f32[640,128]{1,0:T(8,128)} custom-call(s32[1]{0:T(128)} %bitcast.1.odd_ref, f32[640,128]{1,0:T(8,128)} %copy-done.6, f32[640,128]{1,0:T(8,128)} %copy-done.13, f32[640,128]{1,0:T(8,128)} %copy-done.14), custom_call_target="tpu_custom_call" | custom-call | tf_op jit(solution)/shard_map/sum_values/pallas_call | solution.py:322
  80.6 0.0 collective-permute-done.14.far_ref
  80.6 0.7 copy-done.15
  81.3 1.9 %sum_keys.1 = f32[640,128]{1,0:T(8,128)} custom-call(s32[1]{0:T(128)} %bitcast.1.odd_ref, f32[640,128]{1,0:T(8,128)} %copy-done.5, f32[640,128]{1,0:T(8,128)} %copy-done.12, f32[640,128]{1,0:T(8,128)} %copy-done.15), custom_call_target="tpu_custom_call" | custom-call | tf_op jit(solution)/shard_map/sum_keys/pallas_call | solution.py:322
  83.2 0.0 collective-permute-done.11.refs_3_
  83.2 0.0 collective-permute-done.12.refs_5_
  83.3 1.1 %collective-permute-done.13.refs_7_ = f32[32,1024]{1,0:T(8,128)S(1)} collective-permute-done((f32[32,1024]{1,0:T(8,128)S(1)}, f32[32,1024]{1,0:T(8,128)S(1)}, u32[]{:S(2)}, u32[]{:S(2)}) %collective-permute-start.13) | collective-permute-done | bytes 131104 | tf_op jit(solution)/shard_map/ppermute | solution.py:366
  84.4 0.0 copy-done.19
  84.4 0.0 copy-done.20
  84.4 0.0 copy-start.21
  84.4 0.6 copy-done.21
  85.0 2.3 %gather_queries.1 = f32[32,8192]{1,0:T(8,128)} custom-call(s32[1]{0:T(128)} %bitcast.place_ref, f32[32,1024]{1,0:T(8,128)} %copy-done.9, f32[32,1024]{1,0:T(8,128)} %copy-done.10, f32[32,1024]{1,0:T(8,128)} %copy-done.16, f32[32,1024]{1,0:T(8,128)} %copy-done.19, f32[32,1024]{1,0:T(8,128)} %copy-done.17, f32[32,1024]{1,0:T(8,128)} %copy-done.20, ...), custom_call_target="tpu_custom_call" | custom-call | tf_op jit(solution)/shard_map/gather_queries/pallas_call | solution.py:334
  (27 shorter events, 0.2 us)
Async XLA Ops:
  0.6 22.2 %collective-permute-start = (f32[640,128]{1,0:T(8,128)}, f32[640,128]{1,0:T(8,128)S(1)}, u32[]{:S(2)}, u32[]{:S(2)}) collective-permute-start(f32[640,128]{1,0:T(8,128)} %refs_0_.5), channel_id=1, source_target_pairs={{8,0},{12,4},{16,8},{20,12},{24,16},{28,20},{32,24},{36,28},{40,32... | collective-permute-start | bytes 983048 | tf_op jit(solution)/shard_map/ppermute | solution.py:357
  10.5 12.3 %collective-permute-start.1 = (f32[320,128]{1,0:T(8,128)S(1)}, f32[320,128]{1,0:T(8,128)S(1)}, u32[]{:S(2)}, u32[]{:S(2)}) collective-permute-start(f32[320,128]{1,0:T(8,128)S(1)} %slice.6), channel_id=1, source_target_pairs={{8,0},{12,4},{16,8},{20,12},{24,16},{28,20},{32,24},{36,28},{40,32... | collective-permute-start | bytes 491528 | tf_op jit(solution)/shard_map/ppermute | solution.py:357
  11.7 1.2 %copy-start = (f32[128,2048]{1,0:T(8,128)S(1)}, f32[128,2048]{1,0:T(8,128)}, u32[]{:S(2)}) copy-start(f32[128,2048]{1,0:T(8,128)} %q_ref.11) | copy-start | bytes 3145732
  12.9 1.2 %copy-start.1 = (f32[128,2048]{1,0:T(8,128)S(1)}, f32[128,2048]{1,0:T(8,128)}, u32[]{:S(2)}) copy-start(f32[128,2048]{1,0:T(8,128)} %g_ref.11) | copy-start | bytes 3145732
  14.1 1.0 %copy-start.2 = (f32[640,128]{1,0:T(8,128)S(1)}, f32[640,128]{1,0:T(8,128)}, u32[]{:S(2)}) copy-start(f32[640,128]{1,0:T(8,128)} %refs_0_.5) | copy-start | bytes 983044
  15.1 1.0 %copy-start.4 = (f32[640,128]{1,0:T(8,128)S(1)}, f32[640,128]{1,0:T(8,128)}, u32[]{:S(2)}) copy-start(f32[640,128]{1,0:T(8,128)} %refs_2_.1) | copy-start | bytes 983044
  16.1 0.8 copy-start.7
  16.9 0.8 copy-start.11
  22.9 10.7 %collective-permute-start.4 = (f32[320,128]{1,0:T(8,128)S(1)}, f32[320,128]{1,0:T(8,128)S(1)}, u32[]{:S(2)}, u32[]{:S(2)}) collective-permute-start(f32[320,128]{1,0:T(8,128)S(1)} %get-tuple-element.121), channel_id=1, source_target_pairs={{0,4},{4,0},{8,12},{12,8},{16,20},{20,16},{24,28},{28,24},{32,36},... | collective-permute-start | bytes 491528 | tf_op jit(solution)/shard_map/ppermute | solution.py:363
  24.2 4.6 %collective-permute-start.2 = (f32[320,128]{1,0:T(8,128)S(1)}, f32[320,128]{1,0:T(8,128)S(1)}, u32[]{:S(2)}, u32[]{:S(2)}) collective-permute-start(f32[320,128]{1,0:T(8,128)S(1)} %get-tuple-element.122), channel_id=1, source_target_pairs={{8,0},{12,4},{16,8},{20,12},{24,16},{28,20},{32,24},{36,28},{40,32... | collective-permute-start | bytes 491528 | tf_op jit(solution)/shard_map/ppermute | solution.py:357
  26.6 10.7 %collective-permute-start.3 = (f32[640,128]{1,0:T(8,128)S(1)}, f32[640,128]{1,0:T(8,128)S(1)}, u32[]{:S(2)}, u32[]{:S(2)}) collective-permute-start(f32[640,128]{1,0:T(8,128)S(1)} %broadcast_select_fusion), channel_id=1, source_target_pairs={{0,4},{4,0},{8,12},{12,8},{16,20},{20,16},{24,28},{28,24},{32,36},... | collective-permute-start | bytes 983048 | tf_op jit(solution)/shard_map/ppermute | solution.py:363
  28.8 8.4 %collective-permute-start.5 = (f32[320,128]{1,0:T(8,128)S(1)}, f32[320,128]{1,0:T(8,128)S(1)}, u32[]{:S(2)}, u32[]{:S(2)}) collective-permute-start(f32[320,128]{1,0:T(8,128)S(1)} %broadcast_select_fusion.2), channel_id=1, source_target_pairs={{0,4},{4,0},{8,12},{12,8},{16,20},{20,16},{24,28},{28,24},{32,36},... | collective-permute-start | bytes 491528 | tf_op jit(solution)/shard_map/ppermute | solution.py:363
  45.0 8.7 %collective-permute-start.6 = (f32[640,128]{1,0:T(8,128)S(1)}, f32[640,128]{1,0:T(8,128)S(1)}, u32[]{:S(2)}, u32[]{:S(2)}) collective-permute-start(f32[640,128]{1,0:T(8,128)S(1)} %get-tuple-element.79), channel_id=1, source_target_pairs={{0,4},{4,0},{8,12},{12,8},{16,20},{20,16},{24,28},{28,24},{32,36},... | collective-permute-start | bytes 983048 | tf_op jit(solution)/shard_map/ppermute | solution.py:363
  46.9 12.1 %collective-permute-start.10 = (f32[640,128]{1,0:T(8,128)S(1)}, f32[640,128]{1,0:T(8,128)S(1)}, u32[]{:S(2)}, u32[]{:S(2)}) collective-permute-start(f32[640,128]{1,0:T(8,128)S(1)} %get-tuple-element.92), channel_id=1, source_target_pairs={{0,4},{4,0},{8,12},{12,8},{16,20},{20,16},{24,28},{28,24},{32,36},... | collective-permute-start | bytes 983048 | tf_op jit(solution)/shard_map/ppermute | solution.py:363
  47.3 7.8 %copy-start.3 = (f32[640,128]{1,0:T(8,128)S(1)}, f32[640,128]{1,0:T(8,128)}, u32[]{:S(2)}) copy-start(f32[640,128]{1,0:T(8,128)} %refs_0_.5) | copy-start | bytes 983044
  47.3 7.8 %copy-start.8 = (f32[128,128]{1,0:T(8,128)S(1)}, f32[128,128]{1,0:T(8,128)}, u32[]{:S(2)}) copy-start(f32[128,128]{1,0:T(8,128)} %refs_1_.5) | copy-start | bytes 196612
  53.8 5.1 %copy-start.13 = (f32[640,128]{1,0:T(8,128)}, f32[640,128]{1,0:T(8,128)S(1)}, u32[]{:S(2)}) copy-start(f32[640,128]{1,0:T(8,128)S(1)} %collective-permute-done.6.near_ref) | copy-start | bytes 983044
  53.8 24.1 %collective-permute-start.15 = (f32[640,128]{1,0:T(8,128)S(1)}, f32[640,128]{1,0:T(8,128)S(1)}, u32[]{:S(2)}, u32[]{:S(2)}) collective-permute-start(f32[640,128]{1,0:T(8,128)S(1)} %select_add_fusion.1), channel_id=1, source_target_pairs={{0,8},{4,12},{8,16},{12,20},{16,24},{20,28},{24,32},{28,36},{32,40... | collective-permute-start | bytes 983048 | tf_op jit(solution)/shard_map/ppermute | solution.py:360
  58.9 13.1 %copy-start.9 = (f32[32,1024]{1,0:T(8,128)}, f32[32,1024]{1,0:T(8,128)S(1)}, u32[]{:S(2)}) copy-start(f32[32,1024]{1,0:T(8,128)S(1)} %get-tuple-element.102.refs_0_) | copy-start | bytes 393220
  59.0 13.0 %copy-start.12 = (f32[640,128]{1,0:T(8,128)}, f32[640,128]{1,0:T(8,128)S(1)}, u32[]{:S(2)}) copy-start(f32[640,128]{1,0:T(8,128)S(1)} %collective-permute-done.10.near_ref) | copy-start | bytes 983044
  59.1 15.0 %collective-permute-start.7 = (f32[32,1024]{1,0:T(8,128)S(1)}, f32[32,1024]{1,0:T(8,128)S(1)}, u32[]{:S(2)}, u32[]{:S(2)}) collective-permute-start(f32[32,1024]{1,0:T(8,128)S(1)} %get-tuple-element.84), channel_id=1, source_target_pairs={{0,1},{1,0},{2,3},{3,2},{4,5},{5,4},{6,7},{7,6},{8,9},{9,8},{10,11... | collective-permute-start | bytes 393224 | tf_op jit(solution)/shard_map/ppermute | solution.py:366
  64.1 10.0 %collective-permute-start.8 = (f32[32,1024]{1,0:T(8,128)S(1)}, f32[32,1024]{1,0:T(8,128)S(1)}, u32[]{:S(2)}, u32[]{:S(2)}) collective-permute-start(f32[32,1024]{1,0:T(8,128)S(1)} %get-tuple-element.85), channel_id=1, source_target_pairs={{0,2},{1,3},{2,0},{3,1},{4,6},{5,7},{6,4},{7,5},{8,10},{9,11},{10,... | collective-permute-start | bytes 393224 | tf_op jit(solution)/shard_map/ppermute | solution.py:366
  66.9 7.3 %collective-permute-start.9 = (f32[32,1024]{1,0:T(8,128)S(1)}, f32[32,1024]{1,0:T(8,128)S(1)}, u32[]{:S(2)}, u32[]{:S(2)}) collective-permute-start(f32[32,1024]{1,0:T(8,128)S(1)} %get-tuple-element.86), channel_id=1, source_target_pairs={{0,3},{1,2},{2,1},{3,0},{4,7},{5,6},{6,5},{7,4},{8,11},{9,10},{10,... | collective-permute-start | bytes 393224 | tf_op jit(solution)/shard_map/ppermute | solution.py:366
  67.3 13.3 %collective-permute-start.14 = (f32[640,128]{1,0:T(8,128)S(1)}, f32[640,128]{1,0:T(8,128)S(1)}, u32[]{:S(2)}, u32[]{:S(2)}) collective-permute-start(f32[640,128]{1,0:T(8,128)S(1)} %select_add_fusion), channel_id=1, source_target_pairs={{0,8},{4,12},{8,16},{12,20},{16,24},{20,28},{24,32},{28,36},{32,40... | collective-permute-start | bytes 983048 | tf_op jit(solution)/shard_map/ppermute | solution.py:360
  72.0 0.7 copy-start.5
  72.7 0.7 copy-start.6
  73.5 0.6 copy-start.10
  74.1 10.2 %copy-start.16 = (f32[32,1024]{1,0:T(8,128)}, f32[32,1024]{1,0:T(8,128)S(1)}, u32[]{:S(2)}) copy-start(f32[32,1024]{1,0:T(8,128)S(1)} %collective-permute-done.7.refs_2_) | copy-start | bytes 393220
  74.1 10.2 %copy-start.17 = (f32[32,1024]{1,0:T(8,128)}, f32[32,1024]{1,0:T(8,128)S(1)}, u32[]{:S(2)}) copy-start(f32[32,1024]{1,0:T(8,128)S(1)} %collective-permute-done.8.refs_4_) | copy-start | bytes 393220
  74.1 10.2 %copy-start.18 = (f32[32,1024]{1,0:T(8,128)}, f32[32,1024]{1,0:T(8,128)S(1)}, u32[]{:S(2)}) copy-start(f32[32,1024]{1,0:T(8,128)S(1)} %collective-permute-done.9.refs_6_) | copy-start | bytes 393220
  74.1 9.1 %collective-permute-start.11 = (f32[32,1024]{1,0:T(8,128)S(1)}, f32[32,1024]{1,0:T(8,128)S(1)}, u32[]{:S(2)}, u32[]{:S(2)}) collective-permute-start(f32[32,1024]{1,0:T(8,128)S(1)} %get-tuple-element.104), channel_id=1, source_target_pairs={{0,1},{1,0},{2,3},{3,2},{4,5},{5,4},{6,7},{7,6},{8,9},{9,8},{10,11... | collective-permute-start | bytes 393224 | tf_op jit(solution)/shard_map/ppermute | solution.py:366
  74.7 8.6 %collective-permute-start.12 = (f32[32,1024]{1,0:T(8,128)S(1)}, f32[32,1024]{1,0:T(8,128)S(1)}, u32[]{:S(2)}, u32[]{:S(2)}) collective-permute-start(f32[32,1024]{1,0:T(8,128)S(1)} %get-tuple-element.105), channel_id=1, source_target_pairs={{0,2},{1,3},{2,0},{3,1},{4,6},{5,7},{6,4},{7,5},{8,10},{9,11},{10,... | collective-permute-start | bytes 393224 | tf_op jit(solution)/shard_map/ppermute | solution.py:366
  77.4 7.0 %collective-permute-start.13 = (f32[32,1024]{1,0:T(8,128)S(1)}, f32[32,1024]{1,0:T(8,128)S(1)}, u32[]{:S(2)}, u32[]{:S(2)}) collective-permute-start(f32[32,1024]{1,0:T(8,128)S(1)} %get-tuple-element.106), channel_id=1, source_target_pairs={{0,3},{1,2},{2,1},{3,0},{4,7},{5,6},{6,5},{7,4},{8,11},{9,10},{10,... | collective-permute-start | bytes 393224 | tf_op jit(solution)/shard_map/ppermute | solution.py:366
  77.9 0.7 copy-start.14
  80.6 0.7 copy-start.15
  83.2 1.1 %copy-start.19 = (f32[32,1024]{1,0:T(8,128)}, f32[32,1024]{1,0:T(8,128)S(1)}, u32[]{:S(2)}) copy-start(f32[32,1024]{1,0:T(8,128)S(1)} %collective-permute-done.11.refs_3_) | copy-start | bytes 393220
  83.3 1.1 %copy-start.20 = (f32[32,1024]{1,0:T(8,128)}, f32[32,1024]{1,0:T(8,128)S(1)}, u32[]{:S(2)}) copy-start(f32[32,1024]{1,0:T(8,128)S(1)} %collective-permute-done.12.refs_5_) | copy-start | bytes 393220
  84.4 0.7 copy-start.21

commit v2 on v1

--- a/solution.py
+++ b/solution.py
@@ -325,6 +325,7 @@
         in_specs=[SMEM] + blocks,
         out_specs=blocks[0],
         out_shape=shape_of(*own.shape),
+        compiler_params=pltpu.CompilerParams(vmem_limit_bytes=8 * 2**20),
         name=name,
     )(odd, own, near, far)
 
@@ -337,6 +338,7 @@
         in_specs=[SMEM] + whole(parts),
         out_specs=pl.BlockSpec((rows, len(parts) * half), lambda i: (0, 0)),
         out_shape=shape_of(rows, len(parts) * half),
+        compiler_params=pltpu.CompilerParams(vmem_limit_bytes=8 * 2**20),
         name="gather_queries",
     )(place, *parts)
 

time: 87.8 us -> 85.3 us (0.972)
  waiting for transfers between devices: 6.83 us -> 12.6 us
  local copies, waits for them, and re-layouts: 11.2 us -> 7 us
  Pallas kernels: 38.2 us -> 34.5 us
    ppermute x6, waiting for transfers between devices: 1.09 us -> 5.52 us  [exchanged(): lax.ppermute(block, 'head', [(i, i ^ bits) for i in range(head_devices)])]
    unnamed x44 -> x16, local copies, waits for them, and re-layouts: 10.3 us -> 6.07 us
    pallas_call x2, Pallas kernels: 3.88 us -> 1.54 us  [sum_pass(): pl.pallas_call(sum_kernel, grid=(1,), in_specs=[SMEM] + blocks, out_specs...]
    pallas_call x1, Pallas kernels: 2.32 us -> 1.04 us  [gather_pass(): pl.pallas_call(functools.partial(gather_kernel, len(parts) // 2), grid=(1...]
    ppermute x2, waiting for transfers between devices: 0.01 us -> 1.27 us  [to_two_on(): lax.ppermute(block, 'seq', [(i, (i + 2) % count) for i in range(count)])]
  transfers between devices with their start and end apart: 16 -> 16, of which waited for: 4 -> 6; matrix products, arithmetic and copies ran while one was open for 1% -> 1% of each run, Pallas kernels for 32% -> 30%
where the time goes in v2:
time: 85.3 us; the launch traced here: 85 us
  Pallas kernels  34.5 us (40%)
  starting transfers between devices  29.3 us (34%)
  waiting for transfers between devices  12.6 us (15%)
  local copies, waits for them, and re-layouts  7 us (8%)
  between operations  1.41 us (2%)
    pallas_call x3, Pallas kernels, last_pass(): pl.pallas_call(functools.partial(last_kernel, pair, len(keys), len(before...  14.9 us
    ppermute x6, starting transfers between devices, exchanged(): lax.ppermute(block, 'head', [(i, i ^ bits) for i in range(head_devices)])  11.9 us
    ppermute x3, starting transfers between devices, from_two_on(): lax.ppermute(block, 'seq', [((i + 2) % count, i) for i in range(count)])  11.8 us
    pallas_call x2, Pallas kernels, first_pass(): pl.pallas_call(functools.partial(first_kernel, pair, len(keys), len(keys)...  9.22 us
    pallas_call x1, Pallas kernels, middle_pass(): pl.pallas_call(functools.partial(middle_kernel, pair, len(values)), grid=...  7.76 us
    unnamed x16, local copies, waits for them, and re-layouts  6.07 us
    ppermute x6, waiting for transfers between devices, exchanged(): lax.ppermute(block, 'head', [(i, i ^ bits) for i in range(head_devices)])  5.52 us
    ppermute x5, starting transfers between devices, swapped(): return lax.ppermute(block, 'seq', [(i, i ^ 1) for i in range(count)])  4.39 us
  transfers between devices with their start and end apart: 16, of which 6 were waited for; matrix products, arithmetic and copies ran while one was open for 1% of the time, Pallas kernels for 30%

profile of v2, /device:TPU:1, one launch (start us, length us, event | category | flops | bytes accessed | tf_op | source)
XLA Modules:
  0.0 85.0 jit_solution(16956800358745691446)
XLA Ops:
  0.6 8.9 %collective-permute-start = (f32[640,128]{1,0:T(8,128)}, f32[640,128]{1,0:T(8,128)S(1)}, u32[]{:S(2)}, u32[]{:S(2)}) collective-permute-start(f32[640,128]{1,0:T(8,128)} %refs_0_.5), channel_id=1, source_target_pairs={{8,0},{12,4},{16,8},{20,12},{24,16},{28,20},{32,24},{36,28},{40,32... | collective-permute-start | bytes 983048 | tf_op jit(solution)/shard_map/ppermute | solution.py:359
  9.6 0.9 %slice.6 = f32[320,128]{1,0:T(8,128)S(1)} slice(f32[640,128]{1,0:T(8,128)} %refs_2_.1), slice={[0:320], [0:128]} | slice | bytes 327680 | tf_op jit(solution)/shard_map/slice | solution.py:374
  10.5 0.5 collective-permute-start.1
  11.7 0.0 copy-start
  11.7 1.2 %copy-done = f32[128,2048]{1,0:T(8,128)S(1)} copy-done((f32[128,2048]{1,0:T(8,128)S(1)}, f32[128,2048]{1,0:T(8,128)}, u32[]{:S(2)}) %copy-start) | copy-done | bytes 1048600
  12.9 0.0 copy-start.1
  12.9 1.2 %copy-done.1 = f32[128,2048]{1,0:T(8,128)S(1)} copy-done((f32[128,2048]{1,0:T(8,128)S(1)}, f32[128,2048]{1,0:T(8,128)}, u32[]{:S(2)}) %copy-start.1) | copy-done | bytes 1048600
  14.1 0.0 copy-start.2
  14.1 1.0 %copy-done.2 = f32[640,128]{1,0:T(8,128)S(1)} copy-done((f32[640,128]{1,0:T(8,128)S(1)}, f32[640,128]{1,0:T(8,128)}, u32[]{:S(2)}) %copy-start.2) | copy-done | bytes 327704
  15.1 0.0 copy-start.4
  15.1 1.0 %copy-done.4 = f32[640,128]{1,0:T(8,128)S(1)} copy-done((f32[640,128]{1,0:T(8,128)S(1)}, f32[640,128]{1,0:T(8,128)}, u32[]{:S(2)}) %copy-start.4) | copy-done | bytes 327704
  16.1 0.0 copy-start.5
  16.1 0.8 copy-done.5
  16.9 0.0 copy-start.7
  16.9 0.8 copy-done.7
  17.8 5.0 %own_scores.1 = (f32[768,2048]{1,0:T(8,128)S(1)}, f32[768,2048]{1,0:T(8,128)S(1)}, f32[8,2048]{1,0:T(8,128)S(1)}) custom-call(s32[1]{0:T(128)S(6)} %copy.12.length_ref, f32[128,2048]{1,0:T(8,128)S(1)} %copy-done, f32[128,2048]{1,0:T(8,128)S(1)} %copy-done.1, f32[640,128]{1,0:T(8,128)S(1)} %copy-done.2, f32[128,128]{1,0:T(8,128)S(1)} %copy-done.5, ...), custom_call_target="tpu_custom_call" | custom-call | flops 3221225472 | bytes 12582912 | tf_op jit(solution)/shard_map/own_scores/pallas_call | solution.py:251
  22.8 0.0 collective-permute-done.refs_0_
  22.8 0.0 collective-permute-done.1.refs_1_
  22.9 1.3 %collective-permute-start.4 = (f32[320,128]{1,0:T(8,128)S(1)}, f32[320,128]{1,0:T(8,128)S(1)}, u32[]{:S(2)}, u32[]{:S(2)}) collective-permute-start(f32[320,128]{1,0:T(8,128)S(1)} %get-tuple-element.121), channel_id=1, source_target_pairs={{0,4},{4,0},{8,12},{12,8},{16,20},{20,16},{24,28},{28,24},{32,36},... | collective-permute-start | bytes 491528 | tf_op jit(solution)/shard_map/ppermute | solution.py:365
  24.2 2.4 %collective-permute-start.2 = (f32[320,128]{1,0:T(8,128)S(1)}, f32[320,128]{1,0:T(8,128)S(1)}, u32[]{:S(2)}, u32[]{:S(2)}) collective-permute-start(f32[320,128]{1,0:T(8,128)S(1)} %get-tuple-element.122), channel_id=1, source_target_pairs={{8,0},{12,4},{16,8},{20,12},{24,16},{28,20},{32,24},{36,28},{40,32... | collective-permute-start | bytes 491528 | tf_op jit(solution)/shard_map/ppermute | solution.py:359
  26.6 0.3 collective-permute-start.3
  26.9 1.9 %collective-permute-done.2.refs_2_ = f32[320,128]{1,0:T(8,128)S(1)} collective-permute-done((f32[320,128]{1,0:T(8,128)S(1)}, f32[320,128]{1,0:T(8,128)S(1)}, u32[]{:S(2)}, u32[]{:S(2)}) %collective-permute-start.2) | collective-permute-done | bytes 163872 | tf_op jit(solution)/shard_map/ppermute | solution.py:359
  28.8 0.5 collective-permute-start.5
  29.3 4.2 %far_scores.1 = (f32[640,2048]{1,0:T(8,128)S(1)}, f32[640,2048]{1,0:T(8,128)S(1)}, f32[8,2048]{1,0:T(8,128)S(1)}) custom-call(s32[1]{0:T(128)S(6)} %copy.12.length_ref, f32[128,2048]{1,0:T(8,128)S(1)} %copy-done, f32[128,2048]{1,0:T(8,128)S(1)} %copy-done.1, f32[640,128]{1,0:T(8,128)S(1)} %collective-permute-done.refs_0_, ...), custom_call_target="tpu_custom_call" | custom-call | flops 2684354560 | bytes 10485760 | tf_op jit(solution)/shard_map/far_scores/pallas_call | solution.py:251
  33.5 0.0 collective-permute-done.4.refs_0_
  33.5 3.7 %collective-permute-done.5.refs_1_ = f32[320,128]{1,0:T(8,128)S(1)} collective-permute-done((f32[320,128]{1,0:T(8,128)S(1)}, f32[320,128]{1,0:T(8,128)S(1)}, u32[]{:S(2)}, u32[]{:S(2)}) %collective-permute-start.5) | collective-permute-done | bytes 163872 | tf_op jit(solution)/shard_map/ppermute | solution.py:365
  37.2 0.0 collective-permute-done.3.k_ref
  37.3 7.8 %middle_pass.1 = (f32[128,2048]{1,0:T(8,128)S(1)}, f32[8,2048]{1,0:T(8,128)S(1)}, f32[640,128]{1,0:T(8,128)S(1)}, f32[640,128]{1,0:T(8,128)S(1)}) custom-call(s32[1]{0:T(128)S(6)} %copy.12.length_ref, f32[128,2048]{1,0:T(8,128)S(1)} %copy-done, f32[128,2048]{1,0:T(8,128)S(1)} %copy-done.1, f32[8,2048]{1,0:T(8,128)S(1)} %get-tuple-element.69.stats_a, ...), custom_call_target="tpu_custom_call" | custom-call | flops 6710886400 | bytes 5000000 | tf_op jit(solution)/shard_map/middle_pass/pallas_call | solution.py:268
  45.0 1.9 %collective-permute-start.6 = (f32[640,128]{1,0:T(8,128)S(1)}, f32[640,128]{1,0:T(8,128)S(1)}, u32[]{:S(2)}, u32[]{:S(2)}) collective-permute-start(f32[640,128]{1,0:T(8,128)S(1)} %get-tuple-element.79), channel_id=1, source_target_pairs={{0,4},{4,0},{8,12},{12,8},{16,20},{20,16},{24,28},{28,24},{32,36},... | collective-permute-start | bytes 983048 | tf_op jit(solution)/shard_map/ppermute | solution.py:365
  46.9 0.3 collective-permute-start.10
  47.2 0.0 copy-start.3
  47.2 0.0 copy-start.6
  47.2 6.5 %far_grads.1 = (f32[128,2048]{1,0:T(8,128)S(1)}, f32[640,128]{1,0:T(8,128)S(1)}, f32[640,128]{1,0:T(8,128)S(1)}) custom-call(s32[1]{0:T(128)S(6)} %copy.12.length_ref, s32[1]{0:T(128)} %bitcast.place_ref, f32[128,2048]{1,0:T(8,128)S(1)} %copy-done, f32[128,2048]{1,0:T(8,128)S(1)} %copy-done.1, f32[128,2048]{1,0:T(8,128)S(1)} %get-tuple-element.73.before_ref, ...), custom_call_target="tpu_custom_call" | custom-call | flops 4026531840 | bytes 10485760 | tf_op jit(solution)/shard_map/far_grads/pallas_call | solution.py:292
  53.7 0.0 collective-permute-done.6.near_ref
  53.8 1.2 %collective-permute-start.15 = (f32[640,128]{1,0:T(8,128)S(1)}, f32[640,128]{1,0:T(8,128)S(1)}, u32[]{:S(2)}, u32[]{:S(2)}) collective-permute-start(f32[640,128]{1,0:T(8,128)S(1)} %select_add_fusion.1), channel_id=1, source_target_pairs={{0,8},{4,12},{8,16},{12,20},{16,24},{20,28},{24,32},{28,36},{32,40... | collective-permute-start | bytes 983048 | tf_op jit(solution)/shard_map/ppermute | solution.py:362
  55.0 0.0 copy-done.3
  55.0 0.0 copy-done.6
  55.0 3.9 %own_grads_a.1 = (f32[32,1024]{1,0:T(8,128)S(1)}, f32[32,1024]{1,0:T(8,128)S(1)}, f32[32,1024]{1,0:T(8,128)S(1)}, f32[32,1024]{1,0:T(8,128)S(1)}, f32[640,128]{1...) custom-call(s32[1]{0:T(128)S(6)} %copy.12.length_ref, s32[1]{0:T(128)} %bitcast.place_ref, ...), custom_call_target="tpu_custom_call" | custom-call | flops 2415919104 | bytes 6291456 | tf_op jit(solution)/shard_map/own_grads_a/pallas_call | solution.py:292
  58.9 0.2 collective-permute-done.10.near_ref
  59.1 5.0 %collective-permute-start.7 = (f32[32,1024]{1,0:T(8,128)S(1)}, f32[32,1024]{1,0:T(8,128)S(1)}, u32[]{:S(2)}, u32[]{:S(2)}) collective-permute-start(f32[32,1024]{1,0:T(8,128)S(1)} %get-tuple-element.84), channel_id=1, source_target_pairs={{0,1},{1,0},{2,3},{3,2},{4,5},{5,4},{6,7},{7,6},{8,9},{9,8},{10,11... | collective-permute-start | bytes 393224 | tf_op jit(solution)/shard_map/ppermute | solution.py:368
  64.0 2.8 %collective-permute-start.8 = (f32[32,1024]{1,0:T(8,128)S(1)}, f32[32,1024]{1,0:T(8,128)S(1)}, u32[]{:S(2)}, u32[]{:S(2)}) collective-permute-start(f32[32,1024]{1,0:T(8,128)S(1)} %get-tuple-element.85), channel_id=1, source_target_pairs={{0,2},{1,3},{2,0},{3,1},{4,6},{5,7},{6,4},{7,5},{8,10},{9,11},{10,... | collective-permute-start | bytes 393224 | tf_op jit(solution)/shard_map/ppermute | solution.py:368
  66.8 0.5 collective-permute-start.9
  67.3 0.1 collective-permute-start.14
  67.4 4.6 %own_grads_b.1 = (f32[32,1024]{1,0:T(8,128)S(1)}, f32[32,1024]{1,0:T(8,128)S(1)}, f32[32,1024]{1,0:T(8,128)S(1)}, f32[32,1024]{1,0:T(8,128)S(1)}, f32[640,128]{1...) custom-call(s32[1]{0:T(128)S(6)} %copy.12.length_ref, s32[1]{0:T(128)} %bitcast.place_ref, ...), custom_call_target="tpu_custom_call" | custom-call | flops 2415919104 | bytes 6291456 | tf_op jit(solution)/shard_map/own_grads_b/pallas_call | solution.py:292
  71.9 0.0 collective-permute-done.7.refs_2_
  71.9 0.0 collective-permute-done.8.refs_4_
  71.9 2.1 %collective-permute-done.9.refs_6_ = f32[32,1024]{1,0:T(8,128)S(1)} collective-permute-done((f32[32,1024]{1,0:T(8,128)S(1)}, f32[32,1024]{1,0:T(8,128)S(1)}, u32[]{:S(2)}, u32[]{:S(2)}) %collective-permute-start.9) | collective-permute-done | bytes 131104 | tf_op jit(solution)/shard_map/ppermute | solution.py:368
  74.1 0.1 collective-permute-start.11
  74.1 2.4 %collective-permute-start.12 = (f32[32,1024]{1,0:T(8,128)S(1)}, f32[32,1024]{1,0:T(8,128)S(1)}, u32[]{:S(2)}, u32[]{:S(2)}) collective-permute-start(f32[32,1024]{1,0:T(8,128)S(1)} %get-tuple-element.105), channel_id=1, source_target_pairs={{0,2},{1,3},{2,0},{3,1},{4,6},{5,7},{6,4},{7,5},{8,10},{9,11},{10,... | collective-permute-start | bytes 393224 | tf_op jit(solution)/shard_map/ppermute | solution.py:368
  76.5 1.2 %collective-permute-start.13 = (f32[32,1024]{1,0:T(8,128)S(1)}, f32[32,1024]{1,0:T(8,128)S(1)}, u32[]{:S(2)}, u32[]{:S(2)}) collective-permute-start(f32[32,1024]{1,0:T(8,128)S(1)} %get-tuple-element.106), channel_id=1, source_target_pairs={{0,3},{1,2},{2,1},{3,0},{4,7},{5,6},{6,5},{7,4},{8,11},{9,10},{10,... | collective-permute-start | bytes 393224 | tf_op jit(solution)/shard_map/ppermute | solution.py:368
  77.7 0.0 collective-permute-done.15.far_ref
  77.7 0.8 sum_values.1
  78.5 1.3 %collective-permute-done.14.far_ref = f32[640,128]{1,0:T(8,128)S(1)} collective-permute-done((f32[640,128]{1,0:T(8,128)S(1)}, f32[640,128]{1,0:T(8,128)S(1)}, u32[]{:S(2)}, u32[]{:S(2)}) %collective-permute-start.14) | collective-permute-done | bytes 327712 | tf_op jit(solution)/shard_map/ppermute | solution.py:362
  79.8 0.8 sum_keys.1
  80.5 0.0 collective-permute-done.11.refs_3_
  80.5 0.0 collective-permute-done.12.refs_5_
  80.5 3.4 %collective-permute-done.13.refs_7_ = f32[32,1024]{1,0:T(8,128)S(1)} collective-permute-done((f32[32,1024]{1,0:T(8,128)S(1)}, f32[32,1024]{1,0:T(8,128)S(1)}, u32[]{:S(2)}, u32[]{:S(2)}) %collective-permute-start.13) | collective-permute-done | bytes 131104 | tf_op jit(solution)/shard_map/ppermute | solution.py:368
  83.9 1.0 %gather_queries.1 = f32[32,8192]{1,0:T(8,128)} custom-call(s32[1]{0:T(128)} %bitcast.place_ref, f32[32,1024]{1,0:T(8,128)S(1)} %get-tuple-element.102.refs_0_, f32[32,1024]{1,0:T(8,128)S(1)} %get-tuple-element.110.refs_1_, f32[32,1024]{1,0:T(8,128)S(1)} %collective-permute-done.7.refs_2_, f32[32,1024]{1,0:T(8,128)S(1)} %collective-permute-done.11.refs_3_, ...), custom_call_target="tpu_custom_call" | custom-call | tf_op jit(solution)/shard_map/gather_queries/pallas_call | solution.py:335
  (5 shorter events, 0.2 us)
Async XLA Ops:
  0.6 22.2 %collective-permute-start = (f32[640,128]{1,0:T(8,128)}, f32[640,128]{1,0:T(8,128)S(1)}, u32[]{:S(2)}, u32[]{:S(2)}) collective-permute-start(f32[640,128]{1,0:T(8,128)} %refs_0_.5), channel_id=1, source_target_pairs={{8,0},{12,4},{16,8},{20,12},{24,16},{28,20},{32,24},{36,28},{40,32... | collective-permute-start | bytes 983048 | tf_op jit(solution)/shard_map/ppermute | solution.py:359
  10.5 12.3 %collective-permute-start.1 = (f32[320,128]{1,0:T(8,128)S(1)}, f32[320,128]{1,0:T(8,128)S(1)}, u32[]{:S(2)}, u32[]{:S(2)}) collective-permute-start(f32[320,128]{1,0:T(8,128)S(1)} %slice.6), channel_id=1, source_target_pairs={{8,0},{12,4},{16,8},{20,12},{24,16},{28,20},{32,24},{36,28},{40,32... | collective-permute-start | bytes 491528 | tf_op jit(solution)/shard_map/ppermute | solution.py:359
  11.7 1.2 %copy-start = (f32[128,2048]{1,0:T(8,128)S(1)}, f32[128,2048]{1,0:T(8,128)}, u32[]{:S(2)}) copy-start(f32[128,2048]{1,0:T(8,128)} %q_ref.11) | copy-start | bytes 3145732
  12.9 1.2 %copy-start.1 = (f32[128,2048]{1,0:T(8,128)S(1)}, f32[128,2048]{1,0:T(8,128)}, u32[]{:S(2)}) copy-start(f32[128,2048]{1,0:T(8,128)} %g_ref.11) | copy-start | bytes 3145732
  14.1 1.0 %copy-start.2 = (f32[640,128]{1,0:T(8,128)S(1)}, f32[640,128]{1,0:T(8,128)}, u32[]{:S(2)}) copy-start(f32[640,128]{1,0:T(8,128)} %refs_0_.5) | copy-start | bytes 983044
  15.1 1.0 %copy-start.4 = (f32[640,128]{1,0:T(8,128)S(1)}, f32[640,128]{1,0:T(8,128)}, u32[]{:S(2)}) copy-start(f32[640,128]{1,0:T(8,128)} %refs_2_.1) | copy-start | bytes 983044
  16.1 0.8 copy-start.5
  16.9 0.8 copy-start.7
  22.9 10.7 %collective-permute-start.4 = (f32[320,128]{1,0:T(8,128)S(1)}, f32[320,128]{1,0:T(8,128)S(1)}, u32[]{:S(2)}, u32[]{:S(2)}) collective-permute-start(f32[320,128]{1,0:T(8,128)S(1)} %get-tuple-element.121), channel_id=1, source_target_pairs={{0,4},{4,0},{8,12},{12,8},{16,20},{20,16},{24,28},{28,24},{32,36},... | collective-permute-start | bytes 491528 | tf_op jit(solution)/shard_map/ppermute | solution.py:365
  24.2 4.6 %collective-permute-start.2 = (f32[320,128]{1,0:T(8,128)S(1)}, f32[320,128]{1,0:T(8,128)S(1)}, u32[]{:S(2)}, u32[]{:S(2)}) collective-permute-start(f32[320,128]{1,0:T(8,128)S(1)} %get-tuple-element.122), channel_id=1, source_target_pairs={{8,0},{12,4},{16,8},{20,12},{24,16},{28,20},{32,24},{36,28},{40,32... | collective-permute-start | bytes 491528 | tf_op jit(solution)/shard_map/ppermute | solution.py:359
  26.6 10.7 %collective-permute-start.3 = (f32[640,128]{1,0:T(8,128)S(1)}, f32[640,128]{1,0:T(8,128)S(1)}, u32[]{:S(2)}, u32[]{:S(2)}) collective-permute-start(f32[640,128]{1,0:T(8,128)S(1)} %broadcast_select_fusion), channel_id=1, source_target_pairs={{0,4},{4,0},{8,12},{12,8},{16,20},{20,16},{24,28},{28,24},{32,36},... | collective-permute-start | bytes 983048 | tf_op jit(solution)/shard_map/ppermute | solution.py:365
  28.8 8.4 %collective-permute-start.5 = (f32[320,128]{1,0:T(8,128)S(1)}, f32[320,128]{1,0:T(8,128)S(1)}, u32[]{:S(2)}, u32[]{:S(2)}) collective-permute-start(f32[320,128]{1,0:T(8,128)S(1)} %broadcast_select_fusion.2), channel_id=1, source_target_pairs={{0,4},{4,0},{8,12},{12,8},{16,20},{20,16},{24,28},{28,24},{32,36},... | collective-permute-start | bytes 491528 | tf_op jit(solution)/shard_map/ppermute | solution.py:365
  45.0 8.7 %collective-permute-start.6 = (f32[640,128]{1,0:T(8,128)S(1)}, f32[640,128]{1,0:T(8,128)S(1)}, u32[]{:S(2)}, u32[]{:S(2)}) collective-permute-start(f32[640,128]{1,0:T(8,128)S(1)} %get-tuple-element.79), channel_id=1, source_target_pairs={{0,4},{4,0},{8,12},{12,8},{16,20},{20,16},{24,28},{28,24},{32,36},... | collective-permute-start | bytes 983048 | tf_op jit(solution)/shard_map/ppermute | solution.py:365
  46.9 12.1 %collective-permute-start.10 = (f32[640,128]{1,0:T(8,128)S(1)}, f32[640,128]{1,0:T(8,128)S(1)}, u32[]{:S(2)}, u32[]{:S(2)}) collective-permute-start(f32[640,128]{1,0:T(8,128)S(1)} %get-tuple-element.92), channel_id=1, source_target_pairs={{0,4},{4,0},{8,12},{12,8},{16,20},{20,16},{24,28},{28,24},{32,36},... | collective-permute-start | bytes 983048 | tf_op jit(solution)/shard_map/ppermute | solution.py:365
  47.2 7.7 %copy-start.3 = (f32[640,128]{1,0:T(8,128)S(1)}, f32[640,128]{1,0:T(8,128)}, u32[]{:S(2)}) copy-start(f32[640,128]{1,0:T(8,128)} %refs_0_.5) | copy-start | bytes 983044
  47.2 7.7 %copy-start.6 = (f32[128,128]{1,0:T(8,128)S(1)}, f32[128,128]{1,0:T(8,128)}, u32[]{:S(2)}) copy-start(f32[128,128]{1,0:T(8,128)} %refs_1_.5) | copy-start | bytes 196612
  53.8 23.9 %collective-permute-start.15 = (f32[640,128]{1,0:T(8,128)S(1)}, f32[640,128]{1,0:T(8,128)S(1)}, u32[]{:S(2)}, u32[]{:S(2)}) collective-permute-start(f32[640,128]{1,0:T(8,128)S(1)} %select_add_fusion.1), channel_id=1, source_target_pairs={{0,8},{4,12},{8,16},{12,20},{16,24},{20,28},{24,32},{28,36},{32,40... | collective-permute-start | bytes 983048 | tf_op jit(solution)/shard_map/ppermute | solution.py:362
  59.1 12.9 %collective-permute-start.7 = (f32[32,1024]{1,0:T(8,128)S(1)}, f32[32,1024]{1,0:T(8,128)S(1)}, u32[]{:S(2)}, u32[]{:S(2)}) collective-permute-start(f32[32,1024]{1,0:T(8,128)S(1)} %get-tuple-element.84), channel_id=1, source_target_pairs={{0,1},{1,0},{2,3},{3,2},{4,5},{5,4},{6,7},{7,6},{8,9},{9,8},{10,11... | collective-permute-start | bytes 393224 | tf_op jit(solution)/shard_map/ppermute | solution.py:368
  64.0 7.9 %collective-permute-start.8 = (f32[32,1024]{1,0:T(8,128)S(1)}, f32[32,1024]{1,0:T(8,128)S(1)}, u32[]{:S(2)}, u32[]{:S(2)}) collective-permute-start(f32[32,1024]{1,0:T(8,128)S(1)} %get-tuple-element.85), channel_id=1, source_target_pairs={{0,2},{1,3},{2,0},{3,1},{4,6},{5,7},{6,4},{7,5},{8,10},{9,11},{10,... | collective-permute-start | bytes 393224 | tf_op jit(solution)/shard_map/ppermute | solution.py:368
  66.8 7.3 %collective-permute-start.9 = (f32[32,1024]{1,0:T(8,128)S(1)}, f32[32,1024]{1,0:T(8,128)S(1)}, u32[]{:S(2)}, u32[]{:S(2)}) collective-permute-start(f32[32,1024]{1,0:T(8,128)S(1)} %get-tuple-element.86), channel_id=1, source_target_pairs={{0,3},{1,2},{2,1},{3,0},{4,7},{5,6},{6,5},{7,4},{8,11},{9,10},{10,... | collective-permute-start | bytes 393224 | tf_op jit(solution)/shard_map/ppermute | solution.py:368
  67.3 12.5 %collective-permute-start.14 = (f32[640,128]{1,0:T(8,128)S(1)}, f32[640,128]{1,0:T(8,128)S(1)}, u32[]{:S(2)}, u32[]{:S(2)}) collective-permute-start(f32[640,128]{1,0:T(8,128)S(1)} %select_add_fusion), channel_id=1, source_target_pairs={{0,8},{4,12},{8,16},{12,20},{16,24},{20,28},{24,32},{28,36},{32,40... | collective-permute-start | bytes 983048 | tf_op jit(solution)/shard_map/ppermute | solution.py:362
  74.1 6.5 %collective-permute-start.11 = (f32[32,1024]{1,0:T(8,128)S(1)}, f32[32,1024]{1,0:T(8,128)S(1)}, u32[]{:S(2)}, u32[]{:S(2)}) collective-permute-start(f32[32,1024]{1,0:T(8,128)S(1)} %get-tuple-element.104), channel_id=1, source_target_pairs={{0,1},{1,0},{2,3},{3,2},{4,5},{5,4},{6,7},{7,6},{8,9},{9,8},{10,11... | collective-permute-start | bytes 393224 | tf_op jit(solution)/shard_map/ppermute | solution.py:368
  74.1 6.4 %collective-permute-start.12 = (f32[32,1024]{1,0:T(8,128)S(1)}, f32[32,1024]{1,0:T(8,128)S(1)}, u32[]{:S(2)}, u32[]{:S(2)}) collective-permute-start(f32[32,1024]{1,0:T(8,128)S(1)} %get-tuple-element.105), channel_id=1, source_target_pairs={{0,2},{1,3},{2,0},{3,1},{4,6},{5,7},{6,4},{7,5},{8,10},{9,11},{10,... | collective-permute-start | bytes 393224 | tf_op jit(solution)/shard_map/ppermute | solution.py:368
  76.5 7.4 %collective-permute-start.13 = (f32[32,1024]{1,0:T(8,128)S(1)}, f32[32,1024]{1,0:T(8,128)S(1)}, u32[]{:S(2)}, u32[]{:S(2)}) collective-permute-start(f32[32,1024]{1,0:T(8,128)S(1)} %get-tuple-element.106), channel_id=1, source_target_pairs={{0,3},{1,2},{2,1},{3,0},{4,7},{5,6},{6,5},{7,4},{8,11},{9,10},{10,... | collective-permute-start | bytes 393224 | tf_op jit(solution)/shard_map/ppermute | solution.py:368

commit v3 on v2

--- a/solution.py
+++ b/solution.py
@@ -281,7 +281,7 @@
 
 def last_pass(
     lengths, queries, out_grad, place, before, e, dp, final, scale_row, keys, name,
-    first=0, heads=16, before_sums=(), pieces=1, pair=4, step=4,
+    first=0, heads=16, before_sums=(), pieces=1, pair=8, step=8,
 ):
     rows = queries.shape[0]
     total = sum(k.shape[0] for k in keys)

time: 85.3 us -> 84 us (0.985)
  Pallas kernels: 34.5 us -> 30.6 us
  waiting for transfers between devices: 12.6 us -> 15.2 us
    pallas_call x3, Pallas kernels: 14.9 us -> 11 us  [last_pass(): pl.pallas_call(functools.partial(last_kernel, pair, len(keys), len(before...]
    ppermute x5, waiting for transfers between devices: 3.88 us -> 5.82 us  [swapped(): return lax.ppermute(block, 'seq', [(i, i ^ 1) for i in range(count)])]
    ppermute x6, starting transfers between devices: 11.9 us -> 10.6 us  [exchanged(): lax.ppermute(block, 'head', [(i, i ^ bits) for i in range(head_devices)])]
    ppermute x2, starting transfers between devices: 1.26 us -> 2.53 us  [to_two_on(): lax.ppermute(block, 'seq', [(i, (i + 2) % count) for i in range(count)])]
  transfers between devices with their start and end apart: 16 -> 16, of which waited for: 6 -> 6; matrix products, arithmetic and copies ran while one was open for 1% -> 1% of each run, Pallas kernels for 30% -> 26%
where the time goes in v3:
time: 84 us; the launch traced here: 83.7 us
  Pallas kernels  30.6 us (36%)
  starting transfers between devices  29.3 us (35%)
  waiting for transfers between devices  15.2 us (18%)
  local copies, waits for them, and re-layouts  7 us (8%)
  between operations  1.44 us (2%)
    ppermute x3, starting transfers between devices, from_two_on(): lax.ppermute(block, 'seq', [((i + 2) % count, i) for i in range(count)])  11.8 us
    pallas_call x3, Pallas kernels, last_pass(): pl.pallas_call(functools.partial(last_kernel, pair, len(keys), len(before...  11 us
    ppermute x6, starting transfers between devices, exchanged(): lax.ppermute(block, 'head', [(i, i ^ bits) for i in range(head_devices)])  10.6 us
    pallas_call x2, Pallas kernels, first_pass(): pl.pallas_call(functools.partial(first_kernel, pair, len(keys), len(keys)...  9.22 us
    pallas_call x1, Pallas kernels, middle_pass(): pl.pallas_call(functools.partial(middle_kernel, pair, len(values)), grid=...  7.76 us
    ppermute x6, waiting for transfers between devices, exchanged(): lax.ppermute(block, 'head', [(i, i ^ bits) for i in range(head_devices)])  6.17 us
    unnamed x16, local copies, waits for them, and re-layouts  6.07 us
    ppermute x5, waiting for transfers between devices, swapped(): return lax.ppermute(block, 'seq', [(i, i ^ 1) for i in range(count)])  5.82 us
  transfers between devices with their start and end apart: 16, of which 6 were waited for; matrix products, arithmetic and copies ran while one was open for 1% of the time, Pallas kernels for 26%

profile of v3, /device:TPU:1, one launch (start us, length us, event | category | flops | bytes accessed | tf_op | source)
XLA Modules:
  0.0 83.7 jit_solution(3082948331181989965)
XLA Ops:
  0.6 8.9 %collective-permute-start = (f32[640,128]{1,0:T(8,128)}, f32[640,128]{1,0:T(8,128)S(1)}, u32[]{:S(2)}, u32[]{:S(2)}) collective-permute-start(f32[640,128]{1,0:T(8,128)} %refs_0_.5), channel_id=1, source_target_pairs={{8,0},{12,4},{16,8},{20,12},{24,16},{28,20},{32,24},{36,28},{40,32... | collective-permute-start | bytes 983048 | tf_op jit(solution)/shard_map/ppermute | solution.py:359
  9.6 0.9 %slice.6 = f32[320,128]{1,0:T(8,128)S(1)} slice(f32[640,128]{1,0:T(8,128)} %refs_2_.1), slice={[0:320], [0:128]} | slice | bytes 327680 | tf_op jit(solution)/shard_map/slice | solution.py:374
  10.5 0.5 collective-permute-start.1
  11.7 0.0 copy-start
  11.7 1.2 %copy-done = f32[128,2048]{1,0:T(8,128)S(1)} copy-done((f32[128,2048]{1,0:T(8,128)S(1)}, f32[128,2048]{1,0:T(8,128)}, u32[]{:S(2)}) %copy-start) | copy-done | bytes 1048600
  12.9 0.0 copy-start.1
  12.9 1.2 %copy-done.1 = f32[128,2048]{1,0:T(8,128)S(1)} copy-done((f32[128,2048]{1,0:T(8,128)S(1)}, f32[128,2048]{1,0:T(8,128)}, u32[]{:S(2)}) %copy-start.1) | copy-done | bytes 1048600
  14.1 0.0 copy-start.2
  14.1 1.0 %copy-done.2 = f32[640,128]{1,0:T(8,128)S(1)} copy-done((f32[640,128]{1,0:T(8,128)S(1)}, f32[640,128]{1,0:T(8,128)}, u32[]{:S(2)}) %copy-start.2) | copy-done | bytes 327704
  15.1 0.0 copy-start.4
  15.1 1.0 %copy-done.4 = f32[640,128]{1,0:T(8,128)S(1)} copy-done((f32[640,128]{1,0:T(8,128)S(1)}, f32[640,128]{1,0:T(8,128)}, u32[]{:S(2)}) %copy-start.4) | copy-done | bytes 327704
  16.1 0.0 copy-start.5
  16.1 0.8 %copy-done.5 = f32[128,128]{1,0:T(8,128)S(1)} copy-done((f32[128,128]{1,0:T(8,128)S(1)}, f32[128,128]{1,0:T(8,128)}, u32[]{:S(2)}) %copy-start.5) | copy-done | bytes 65560
  16.9 0.0 copy-start.7
  16.9 0.8 %copy-done.7 = f32[128,128]{1,0:T(8,128)S(1)} copy-done((f32[128,128]{1,0:T(8,128)S(1)}, f32[128,128]{1,0:T(8,128)}, u32[]{:S(2)}) %copy-start.7) | copy-done | bytes 65560
  17.8 5.0 %own_scores.1 = (f32[768,2048]{1,0:T(8,128)S(1)}, f32[768,2048]{1,0:T(8,128)S(1)}, f32[8,2048]{1,0:T(8,128)S(1)}) custom-call(s32[1]{0:T(128)S(6)} %copy.12.length_ref, f32[128,2048]{1,0:T(8,128)S(1)} %copy-done, f32[128,2048]{1,0:T(8,128)S(1)} %copy-done.1, f32[640,128]{1,0:T(8,128)S(1)} %copy-done.2, f32[128,128]{1,0:T(8,128)S(1)} %copy-done.5, ...), custom_call_target="tpu_custom_call" | custom-call | flops 3221225472 | bytes 12582912 | tf_op jit(solution)/shard_map/own_scores/pallas_call | solution.py:251
  22.8 0.0 collective-permute-done.refs_0_
  22.8 0.0 collective-permute-done.1.refs_1_
  22.9 1.3 %collective-permute-start.4 = (f32[320,128]{1,0:T(8,128)S(1)}, f32[320,128]{1,0:T(8,128)S(1)}, u32[]{:S(2)}, u32[]{:S(2)}) collective-permute-start(f32[320,128]{1,0:T(8,128)S(1)} %get-tuple-element.121), channel_id=1, source_target_pairs={{0,4},{4,0},{8,12},{12,8},{16,20},{20,16},{24,28},{28,24},{32,36},... | collective-permute-start | bytes 491528 | tf_op jit(solution)/shard_map/ppermute | solution.py:365
  24.2 2.4 %collective-permute-start.2 = (f32[320,128]{1,0:T(8,128)S(1)}, f32[320,128]{1,0:T(8,128)S(1)}, u32[]{:S(2)}, u32[]{:S(2)}) collective-permute-start(f32[320,128]{1,0:T(8,128)S(1)} %get-tuple-element.122), channel_id=1, source_target_pairs={{8,0},{12,4},{16,8},{20,12},{24,16},{28,20},{32,24},{36,28},{40,32... | collective-permute-start | bytes 491528 | tf_op jit(solution)/shard_map/ppermute | solution.py:359
  26.6 0.3 collective-permute-start.3
  26.9 1.9 %collective-permute-done.2.refs_2_ = f32[320,128]{1,0:T(8,128)S(1)} collective-permute-done((f32[320,128]{1,0:T(8,128)S(1)}, f32[320,128]{1,0:T(8,128)S(1)}, u32[]{:S(2)}, u32[]{:S(2)}) %collective-permute-start.2) | collective-permute-done | bytes 163872 | tf_op jit(solution)/shard_map/ppermute | solution.py:359
  28.8 0.5 collective-permute-start.5
  29.3 4.2 %far_scores.1 = (f32[640,2048]{1,0:T(8,128)S(1)}, f32[640,2048]{1,0:T(8,128)S(1)}, f32[8,2048]{1,0:T(8,128)S(1)}) custom-call(s32[1]{0:T(128)S(6)} %copy.12.length_ref, f32[128,2048]{1,0:T(8,128)S(1)} %copy-done, f32[128,2048]{1,0:T(8,128)S(1)} %copy-done.1, f32[640,128]{1,0:T(8,128)S(1)} %collective-permute-done.refs_0_, ...), custom_call_target="tpu_custom_call" | custom-call | flops 2684354560 | bytes 10485760 | tf_op jit(solution)/shard_map/far_scores/pallas_call | solution.py:251
  33.5 0.0 collective-permute-done.4.refs_0_
  33.5 3.7 %collective-permute-done.5.refs_1_ = f32[320,128]{1,0:T(8,128)S(1)} collective-permute-done((f32[320,128]{1,0:T(8,128)S(1)}, f32[320,128]{1,0:T(8,128)S(1)}, u32[]{:S(2)}, u32[]{:S(2)}) %collective-permute-start.5) | collective-permute-done | bytes 163872 | tf_op jit(solution)/shard_map/ppermute | solution.py:365
  37.2 0.0 collective-permute-done.3.k_ref
  37.3 7.8 %middle_pass.1 = (f32[128,2048]{1,0:T(8,128)S(1)}, f32[8,2048]{1,0:T(8,128)S(1)}, f32[640,128]{1,0:T(8,128)S(1)}, f32[640,128]{1,0:T(8,128)S(1)}) custom-call(s32[1]{0:T(128)S(6)} %copy.12.length_ref, f32[128,2048]{1,0:T(8,128)S(1)} %copy-done, f32[128,2048]{1,0:T(8,128)S(1)} %copy-done.1, f32[8,2048]{1,0:T(8,128)S(1)} %get-tuple-element.69.stats_a, ...), custom_call_target="tpu_custom_call" | custom-call | flops 6710886400 | bytes 5000000 | tf_op jit(solution)/shard_map/middle_pass/pallas_call | solution.py:268
  45.0 1.9 %collective-permute-start.6 = (f32[640,128]{1,0:T(8,128)S(1)}, f32[640,128]{1,0:T(8,128)S(1)}, u32[]{:S(2)}, u32[]{:S(2)}) collective-permute-start(f32[640,128]{1,0:T(8,128)S(1)} %get-tuple-element.79), channel_id=1, source_target_pairs={{0,4},{4,0},{8,12},{12,8},{16,20},{20,16},{24,28},{28,24},{32,36},... | collective-permute-start | bytes 983048 | tf_op jit(solution)/shard_map/ppermute | solution.py:365
  46.9 0.3 collective-permute-start.10
  47.2 0.0 copy-start.3
  47.2 0.0 copy-start.6
  47.2 5.8 %far_grads.1 = (f32[128,2048]{1,0:T(8,128)S(1)}, f32[640,128]{1,0:T(8,128)S(1)}, f32[640,128]{1,0:T(8,128)S(1)}) custom-call(s32[1]{0:T(128)S(6)} %copy.12.length_ref, s32[1]{0:T(128)} %bitcast.place_ref, f32[128,2048]{1,0:T(8,128)S(1)} %copy-done, f32[128,2048]{1,0:T(8,128)S(1)} %copy-done.1, f32[128,2048]{1,0:T(8,128)S(1)} %get-tuple-element.73.before_ref, ...), custom_call_target="tpu_custom_call" | custom-call | flops 4026531840 | bytes 10485760 | tf_op jit(solution)/shard_map/far_grads/pallas_call | solution.py:292
  53.1 0.0 collective-permute-done.6.near_ref
  53.1 1.2 %collective-permute-start.15 = (f32[640,128]{1,0:T(8,128)S(1)}, f32[640,128]{1,0:T(8,128)S(1)}, u32[]{:S(2)}, u32[]{:S(2)}) collective-permute-start(f32[640,128]{1,0:T(8,128)S(1)} %select_add_fusion.1), channel_id=1, source_target_pairs={{0,8},{4,12},{8,16},{12,20},{16,24},{20,28},{24,32},{28,36},{32,40... | collective-permute-start | bytes 983048 | tf_op jit(solution)/shard_map/ppermute | solution.py:362
  54.3 0.0 copy-done.3
  54.3 0.0 copy-done.6
  54.3 2.6 %own_grads_a.1 = (f32[32,1024]{1,0:T(8,128)S(1)}, f32[32,1024]{1,0:T(8,128)S(1)}, f32[32,1024]{1,0:T(8,128)S(1)}, f32[32,1024]{1,0:T(8,128)S(1)}, f32[640,128]{1...) custom-call(s32[1]{0:T(128)S(6)} %copy.12.length_ref, s32[1]{0:T(128)} %bitcast.place_ref, ...), custom_call_target="tpu_custom_call" | custom-call | flops 2415919104 | bytes 6291456 | tf_op jit(solution)/shard_map/own_grads_a/pallas_call | solution.py:292
  56.9 2.1 %collective-permute-done.10.near_ref = f32[640,128]{1,0:T(8,128)S(1)} collective-permute-done((f32[640,128]{1,0:T(8,128)S(1)}, f32[640,128]{1,0:T(8,128)S(1)}, u32[]{:S(2)}, u32[]{:S(2)}) %collective-permute-start.10) | collective-permute-done | bytes 327712 | tf_op jit(solution)/shard_map/ppermute | solution.py:365
  59.1 3.7 %collective-permute-start.7 = (f32[32,1024]{1,0:T(8,128)S(1)}, f32[32,1024]{1,0:T(8,128)S(1)}, u32[]{:S(2)}, u32[]{:S(2)}) collective-permute-start(f32[32,1024]{1,0:T(8,128)S(1)} %get-tuple-element.84), channel_id=1, source_target_pairs={{0,1},{1,0},{2,3},{3,2},{4,5},{5,4},{6,7},{7,6},{8,9},{9,8},{10,11... | collective-permute-start | bytes 393224 | tf_op jit(solution)/shard_map/ppermute | solution.py:368
  62.8 2.8 %collective-permute-start.8 = (f32[32,1024]{1,0:T(8,128)S(1)}, f32[32,1024]{1,0:T(8,128)S(1)}, u32[]{:S(2)}, u32[]{:S(2)}) collective-permute-start(f32[32,1024]{1,0:T(8,128)S(1)} %get-tuple-element.85), channel_id=1, source_target_pairs={{0,2},{1,3},{2,0},{3,1},{4,6},{5,7},{6,4},{7,5},{8,10},{9,11},{10,... | collective-permute-start | bytes 393224 | tf_op jit(solution)/shard_map/ppermute | solution.py:368
  65.5 0.5 collective-permute-start.9
  66.0 1.4 %collective-permute-start.14 = (f32[640,128]{1,0:T(8,128)S(1)}, f32[640,128]{1,0:T(8,128)S(1)}, u32[]{:S(2)}, u32[]{:S(2)}) collective-permute-start(f32[640,128]{1,0:T(8,128)S(1)} %select_add_fusion), channel_id=1, source_target_pairs={{0,8},{4,12},{8,16},{12,20},{16,24},{20,28},{24,32},{28,36},{32,40... | collective-permute-start | bytes 983048 | tf_op jit(solution)/shard_map/ppermute | solution.py:362
  67.4 2.6 %own_grads_b.1 = (f32[32,1024]{1,0:T(8,128)S(1)}, f32[32,1024]{1,0:T(8,128)S(1)}, f32[32,1024]{1,0:T(8,128)S(1)}, f32[32,1024]{1,0:T(8,128)S(1)}, f32[640,128]{1...) custom-call(s32[1]{0:T(128)S(6)} %copy.12.length_ref, s32[1]{0:T(128)} %bitcast.place_ref, ...), custom_call_target="tpu_custom_call" | custom-call | flops 2415919104 | bytes 6291456 | tf_op jit(solution)/shard_map/own_grads_b/pallas_call | solution.py:292
  70.0 0.0 collective-permute-done.7.refs_2_
  70.0 0.0 collective-permute-done.8.refs_4_
  70.0 2.8 %collective-permute-done.9.refs_6_ = f32[32,1024]{1,0:T(8,128)S(1)} collective-permute-done((f32[32,1024]{1,0:T(8,128)S(1)}, f32[32,1024]{1,0:T(8,128)S(1)}, u32[]{:S(2)}, u32[]{:S(2)}) %collective-permute-start.9) | collective-permute-done | bytes 131104 | tf_op jit(solution)/shard_map/ppermute | solution.py:368
  72.8 0.1 collective-permute-start.11
  72.8 2.4 %collective-permute-start.12 = (f32[32,1024]{1,0:T(8,128)S(1)}, f32[32,1024]{1,0:T(8,128)S(1)}, u32[]{:S(2)}, u32[]{:S(2)}) collective-permute-start(f32[32,1024]{1,0:T(8,128)S(1)} %get-tuple-element.105), channel_id=1, source_target_pairs={{0,2},{1,3},{2,0},{3,1},{4,6},{5,7},{6,4},{7,5},{8,10},{9,11},{10,... | collective-permute-start | bytes 393224 | tf_op jit(solution)/shard_map/ppermute | solution.py:368
  75.3 1.2 %collective-permute-start.13 = (f32[32,1024]{1,0:T(8,128)S(1)}, f32[32,1024]{1,0:T(8,128)S(1)}, u32[]{:S(2)}, u32[]{:S(2)}) collective-permute-start(f32[32,1024]{1,0:T(8,128)S(1)} %get-tuple-element.106), channel_id=1, source_target_pairs={{0,3},{1,2},{2,1},{3,0},{4,7},{5,6},{6,5},{7,4},{8,11},{9,10},{10,... | collective-permute-start | bytes 393224 | tf_op jit(solution)/shard_map/ppermute | solution.py:368
  76.4 0.0 collective-permute-done.15.far_ref
  76.4 0.8 sum_values.1
  77.2 1.3 %collective-permute-done.14.far_ref = f32[640,128]{1,0:T(8,128)S(1)} collective-permute-done((f32[640,128]{1,0:T(8,128)S(1)}, f32[640,128]{1,0:T(8,128)S(1)}, u32[]{:S(2)}, u32[]{:S(2)}) %collective-permute-start.14) | collective-permute-done | bytes 327712 | tf_op jit(solution)/shard_map/ppermute | solution.py:362
  78.5 0.8 sum_keys.1
  79.2 0.0 collective-permute-done.11.refs_3_
  79.3 0.0 collective-permute-done.12.refs_5_
  79.3 3.4 %collective-permute-done.13.refs_7_ = f32[32,1024]{1,0:T(8,128)S(1)} collective-permute-done((f32[32,1024]{1,0:T(8,128)S(1)}, f32[32,1024]{1,0:T(8,128)S(1)}, u32[]{:S(2)}, u32[]{:S(2)}) %collective-permute-start.13) | collective-permute-done | bytes 131104 | tf_op jit(solution)/shard_map/ppermute | solution.py:368
  82.6 1.0 %gather_queries.1 = f32[32,8192]{1,0:T(8,128)} custom-call(s32[1]{0:T(128)} %bitcast.place_ref, f32[32,1024]{1,0:T(8,128)S(1)} %get-tuple-element.102.refs_0_, f32[32,1024]{1,0:T(8,128)S(1)} %get-tuple-element.110.refs_1_, f32[32,1024]{1,0:T(8,128)S(1)} %collective-permute-done.7.refs_2_, f32[32,1024]{1,0:T(8,128)S(1)} %collective-permute-done.11.refs_3_, ...), custom_call_target="tpu_custom_call" | custom-call | tf_op jit(solution)/shard_map/gather_queries/pallas_call | solution.py:335
  (5 shorter events, 0.2 us)
Async XLA Ops:
  0.6 22.2 %collective-permute-start = (f32[640,128]{1,0:T(8,128)}, f32[640,128]{1,0:T(8,128)S(1)}, u32[]{:S(2)}, u32[]{:S(2)}) collective-permute-start(f32[640,128]{1,0:T(8,128)} %refs_0_.5), channel_id=1, source_target_pairs={{8,0},{12,4},{16,8},{20,12},{24,16},{28,20},{32,24},{36,28},{40,32... | collective-permute-start | bytes 983048 | tf_op jit(solution)/shard_map/ppermute | solution.py:359
  10.5 12.3 %collective-permute-start.1 = (f32[320,128]{1,0:T(8,128)S(1)}, f32[320,128]{1,0:T(8,128)S(1)}, u32[]{:S(2)}, u32[]{:S(2)}) collective-permute-start(f32[320,128]{1,0:T(8,128)S(1)} %slice.6), channel_id=1, source_target_pairs={{8,0},{12,4},{16,8},{20,12},{24,16},{28,20},{32,24},{36,28},{40,32... | collective-permute-start | bytes 491528 | tf_op jit(solution)/shard_map/ppermute | solution.py:359
  11.7 1.2 %copy-start = (f32[128,2048]{1,0:T(8,128)S(1)}, f32[128,2048]{1,0:T(8,128)}, u32[]{:S(2)}) copy-start(f32[128,2048]{1,0:T(8,128)} %q_ref.11) | copy-start | bytes 3145732
  12.9 1.2 %copy-start.1 = (f32[128,2048]{1,0:T(8,128)S(1)}, f32[128,2048]{1,0:T(8,128)}, u32[]{:S(2)}) copy-start(f32[128,2048]{1,0:T(8,128)} %g_ref.11) | copy-start | bytes 3145732
  14.1 1.0 %copy-start.2 = (f32[640,128]{1,0:T(8,128)S(1)}, f32[640,128]{1,0:T(8,128)}, u32[]{:S(2)}) copy-start(f32[640,128]{1,0:T(8,128)} %refs_0_.5) | copy-start | bytes 983044
  15.1 1.0 %copy-start.4 = (f32[640,128]{1,0:T(8,128)S(1)}, f32[640,128]{1,0:T(8,128)}, u32[]{:S(2)}) copy-start(f32[640,128]{1,0:T(8,128)} %refs_2_.1) | copy-start | bytes 983044
  16.1 0.8 %copy-start.5 = (f32[128,128]{1,0:T(8,128)S(1)}, f32[128,128]{1,0:T(8,128)}, u32[]{:S(2)}) copy-start(f32[128,128]{1,0:T(8,128)} %refs_1_.5) | copy-start | bytes 196612
  16.9 0.8 %copy-start.7 = (f32[128,128]{1,0:T(8,128)S(1)}, f32[128,128]{1,0:T(8,128)}, u32[]{:S(2)}) copy-start(f32[128,128]{1,0:T(8,128)} %refs_3_.1) | copy-start | bytes 196612
  22.9 10.7 %collective-permute-start.4 = (f32[320,128]{1,0:T(8,128)S(1)}, f32[320,128]{1,0:T(8,128)S(1)}, u32[]{:S(2)}, u32[]{:S(2)}) collective-permute-start(f32[320,128]{1,0:T(8,128)S(1)} %get-tuple-element.121), channel_id=1, source_target_pairs={{0,4},{4,0},{8,12},{12,8},{16,20},{20,16},{24,28},{28,24},{32,36},... | collective-permute-start | bytes 491528 | tf_op jit(solution)/shard_map/ppermute | solution.py:365
  24.2 4.6 %collective-permute-start.2 = (f32[320,128]{1,0:T(8,128)S(1)}, f32[320,128]{1,0:T(8,128)S(1)}, u32[]{:S(2)}, u32[]{:S(2)}) collective-permute-start(f32[320,128]{1,0:T(8,128)S(1)} %get-tuple-element.122), channel_id=1, source_target_pairs={{8,0},{12,4},{16,8},{20,12},{24,16},{28,20},{32,24},{36,28},{40,32... | collective-permute-start | bytes 491528 | tf_op jit(solution)/shard_map/ppermute | solution.py:359
  26.6 10.7 %collective-permute-start.3 = (f32[640,128]{1,0:T(8,128)S(1)}, f32[640,128]{1,0:T(8,128)S(1)}, u32[]{:S(2)}, u32[]{:S(2)}) collective-permute-start(f32[640,128]{1,0:T(8,128)S(1)} %broadcast_select_fusion), channel_id=1, source_target_pairs={{0,4},{4,0},{8,12},{12,8},{16,20},{20,16},{24,28},{28,24},{32,36},... | collective-permute-start | bytes 983048 | tf_op jit(solution)/shard_map/ppermute | solution.py:365
  28.8 8.4 %collective-permute-start.5 = (f32[320,128]{1,0:T(8,128)S(1)}, f32[320,128]{1,0:T(8,128)S(1)}, u32[]{:S(2)}, u32[]{:S(2)}) collective-permute-start(f32[320,128]{1,0:T(8,128)S(1)} %broadcast_select_fusion.2), channel_id=1, source_target_pairs={{0,4},{4,0},{8,12},{12,8},{16,20},{20,16},{24,28},{28,24},{32,36},... | collective-permute-start | bytes 491528 | tf_op jit(solution)/shard_map/ppermute | solution.py:365
  45.0 8.1 %collective-permute-start.6 = (f32[640,128]{1,0:T(8,128)S(1)}, f32[640,128]{1,0:T(8,128)S(1)}, u32[]{:S(2)}, u32[]{:S(2)}) collective-permute-start(f32[640,128]{1,0:T(8,128)S(1)} %get-tuple-element.79), channel_id=1, source_target_pairs={{0,4},{4,0},{8,12},{12,8},{16,20},{20,16},{24,28},{28,24},{32,36},... | collective-permute-start | bytes 983048 | tf_op jit(solution)/shard_map/ppermute | solution.py:365
  46.9 12.1 %collective-permute-start.10 = (f32[640,128]{1,0:T(8,128)S(1)}, f32[640,128]{1,0:T(8,128)S(1)}, u32[]{:S(2)}, u32[]{:S(2)}) collective-permute-start(f32[640,128]{1,0:T(8,128)S(1)} %get-tuple-element.92), channel_id=1, source_target_pairs={{0,4},{4,0},{8,12},{12,8},{16,20},{20,16},{24,28},{28,24},{32,36},... | collective-permute-start | bytes 983048 | tf_op jit(solution)/shard_map/ppermute | solution.py:365
  47.2 7.1 %copy-start.3 = (f32[640,128]{1,0:T(8,128)S(1)}, f32[640,128]{1,0:T(8,128)}, u32[]{:S(2)}) copy-start(f32[640,128]{1,0:T(8,128)} %refs_0_.5) | copy-start | bytes 983044
  47.2 7.1 %copy-start.6 = (f32[128,128]{1,0:T(8,128)S(1)}, f32[128,128]{1,0:T(8,128)}, u32[]{:S(2)}) copy-start(f32[128,128]{1,0:T(8,128)} %refs_1_.5) | copy-start | bytes 196612
  53.1 23.3 %collective-permute-start.15 = (f32[640,128]{1,0:T(8,128)S(1)}, f32[640,128]{1,0:T(8,128)S(1)}, u32[]{:S(2)}, u32[]{:S(2)}) collective-permute-start(f32[640,128]{1,0:T(8,128)S(1)} %select_add_fusion.1), channel_id=1, source_target_pairs={{0,8},{4,12},{8,16},{12,20},{16,24},{20,28},{24,32},{28,36},{32,40... | collective-permute-start | bytes 983048 | tf_op jit(solution)/shard_map/ppermute | solution.py:362
  59.1 10.9 %collective-permute-start.7 = (f32[32,1024]{1,0:T(8,128)S(1)}, f32[32,1024]{1,0:T(8,128)S(1)}, u32[]{:S(2)}, u32[]{:S(2)}) collective-permute-start(f32[32,1024]{1,0:T(8,128)S(1)} %get-tuple-element.84), channel_id=1, source_target_pairs={{0,1},{1,0},{2,3},{3,2},{4,5},{5,4},{6,7},{7,6},{8,9},{9,8},{10,11... | collective-permute-start | bytes 393224 | tf_op jit(solution)/shard_map/ppermute | solution.py:368
  62.8 7.2 %collective-permute-start.8 = (f32[32,1024]{1,0:T(8,128)S(1)}, f32[32,1024]{1,0:T(8,128)S(1)}, u32[]{:S(2)}, u32[]{:S(2)}) collective-permute-start(f32[32,1024]{1,0:T(8,128)S(1)} %get-tuple-element.85), channel_id=1, source_target_pairs={{0,2},{1,3},{2,0},{3,1},{4,6},{5,7},{6,4},{7,5},{8,10},{9,11},{10,... | collective-permute-start | bytes 393224 | tf_op jit(solution)/shard_map/ppermute | solution.py:368
  65.5 7.3 %collective-permute-start.9 = (f32[32,1024]{1,0:T(8,128)S(1)}, f32[32,1024]{1,0:T(8,128)S(1)}, u32[]{:S(2)}, u32[]{:S(2)}) collective-permute-start(f32[32,1024]{1,0:T(8,128)S(1)} %get-tuple-element.86), channel_id=1, source_target_pairs={{0,3},{1,2},{2,1},{3,0},{4,7},{5,6},{6,5},{7,4},{8,11},{9,10},{10,... | collective-permute-start | bytes 393224 | tf_op jit(solution)/shard_map/ppermute | solution.py:368
  66.0 12.5 %collective-permute-start.14 = (f32[640,128]{1,0:T(8,128)S(1)}, f32[640,128]{1,0:T(8,128)S(1)}, u32[]{:S(2)}, u32[]{:S(2)}) collective-permute-start(f32[640,128]{1,0:T(8,128)S(1)} %select_add_fusion), channel_id=1, source_target_pairs={{0,8},{4,12},{8,16},{12,20},{16,24},{20,28},{24,32},{28,36},{32,40... | collective-permute-start | bytes 983048 | tf_op jit(solution)/shard_map/ppermute | solution.py:362
  72.8 6.5 %collective-permute-start.11 = (f32[32,1024]{1,0:T(8,128)S(1)}, f32[32,1024]{1,0:T(8,128)S(1)}, u32[]{:S(2)}, u32[]{:S(2)}) collective-permute-start(f32[32,1024]{1,0:T(8,128)S(1)} %get-tuple-element.104), channel_id=1, source_target_pairs={{0,1},{1,0},{2,3},{3,2},{4,5},{5,4},{6,7},{7,6},{8,9},{9,8},{10,11... | collective-permute-start | bytes 393224 | tf_op jit(solution)/shard_map/ppermute | solution.py:368
  72.8 6.4 %collective-permute-start.12 = (f32[32,1024]{1,0:T(8,128)S(1)}, f32[32,1024]{1,0:T(8,128)S(1)}, u32[]{:S(2)}, u32[]{:S(2)}) collective-permute-start(f32[32,1024]{1,0:T(8,128)S(1)} %get-tuple-element.105), channel_id=1, source_target_pairs={{0,2},{1,3},{2,0},{3,1},{4,6},{5,7},{6,4},{7,5},{8,10},{9,11},{10,... | collective-permute-start | bytes 393224 | tf_op jit(solution)/shard_map/ppermute | solution.py:368
  75.3 7.4 %collective-permute-start.13 = (f32[32,1024]{1,0:T(8,128)S(1)}, f32[32,1024]{1,0:T(8,128)S(1)}, u32[]{:S(2)}, u32[]{:S(2)}) collective-permute-start(f32[32,1024]{1,0:T(8,128)S(1)} %get-tuple-element.106), channel_id=1, source_target_pairs={{0,3},{1,2},{2,1},{3,0},{4,7},{5,6},{6,5},{7,4},{8,11},{9,10},{10,... | collective-permute-start | bytes 393224 | tf_op jit(solution)/shard_map/ppermute | solution.py:368

commit v4 on v3

--- a/solution.py
+++ b/solution.py
@@ -260,7 +260,7 @@
     )(lengths, queries, out_grad, *keys, *values)
 
 
-def middle_pass(lengths, queries, out_grad, stats_a, stats_b, key_block, values, pair=8, step=16):
+def middle_pass(lengths, queries, out_grad, stats_a, stats_b, key_block, values, pair=16, step=16):
     rows, width = queries.shape
     total = key_block.shape[0]
     slots = rows * width // SIZE

time: 84 us -> 83.6 us (level)
  no operation moved by 1% of the time
where the time goes in v4:
time: 83.6 us; the launch traced here: 83.2 us
  Pallas kernels  30.1 us (36%)
  starting transfers between devices  29.3 us (35%)
  waiting for transfers between devices  15.2 us (18%)
  local copies, waits for them, and re-layouts  7 us (8%)
  between operations  1.44 us (2%)
    ppermute x3, starting transfers between devices, from_two_on(): lax.ppermute(block, 'seq', [((i + 2) % count, i) for i in range(count)])  11.8 us
    pallas_call x3, Pallas kernels, last_pass(): pl.pallas_call(functools.partial(last_kernel, pair, len(keys), len(before...  11 us
    ppermute x6, starting transfers between devices, exchanged(): lax.ppermute(block, 'head', [(i, i ^ bits) for i in range(head_devices)])  10.6 us
    pallas_call x2, Pallas kernels, first_pass(): pl.pallas_call(functools.partial(first_kernel, pair, len(keys), len(keys)...  9.22 us
    pallas_call x1, Pallas kernels, middle_pass(): pl.pallas_call(functools.partial(middle_kernel, pair, len(values)), grid=...  7.31 us
    ppermute x6, waiting for transfers between devices, exchanged(): lax.ppermute(block, 'head', [(i, i ^ bits) for i in range(head_devices)])  6.18 us
    unnamed x16, local copies, waits for them, and re-layouts  6.07 us
    ppermute x5, waiting for transfers between devices, swapped(): return lax.ppermute(block, 'seq', [(i, i ^ 1) for i in range(count)])  5.82 us
  transfers between devices with their start and end apart: 16, of which 6 were waited for; matrix products, arithmetic and copies ran while one was open for 1% of the time, Pallas kernels for 26%

profile of v4, /device:TPU:1, one launch (start us, length us, event | category | flops | bytes accessed | tf_op | source)
XLA Modules:
  0.0 83.2 jit_solution(14732224108753721392)
XLA Ops:
  0.6 8.9 %collective-permute-start = (f32[640,128]{1,0:T(8,128)}, f32[640,128]{1,0:T(8,128)S(1)}, u32[]{:S(2)}, u32[]{:S(2)}) collective-permute-start(f32[640,128]{1,0:T(8,128)} %refs_0_.5), channel_id=1, source_target_pairs={{8,0},{12,4},{16,8},{20,12},{24,16},{28,20},{32,24},{36,28},{40,32... | collective-permute-start | bytes 983048 | tf_op jit(solution)/shard_map/ppermute | solution.py:359
  9.6 0.9 %slice.6 = f32[320,128]{1,0:T(8,128)S(1)} slice(f32[640,128]{1,0:T(8,128)} %refs_2_.1), slice={[0:320], [0:128]} | slice | bytes 327680 | tf_op jit(solution)/shard_map/slice | solution.py:374
  10.5 0.5 collective-permute-start.1
  11.7 0.0 copy-start
  11.7 1.2 %copy-done = f32[128,2048]{1,0:T(8,128)S(1)} copy-done((f32[128,2048]{1,0:T(8,128)S(1)}, f32[128,2048]{1,0:T(8,128)}, u32[]{:S(2)}) %copy-start) | copy-done | bytes 1048600
  12.9 0.0 copy-start.1
  12.9 1.2 %copy-done.1 = f32[128,2048]{1,0:T(8,128)S(1)} copy-done((f32[128,2048]{1,0:T(8,128)S(1)}, f32[128,2048]{1,0:T(8,128)}, u32[]{:S(2)}) %copy-start.1) | copy-done | bytes 1048600
  14.1 0.0 copy-start.2
  14.1 1.0 %copy-done.2 = f32[640,128]{1,0:T(8,128)S(1)} copy-done((f32[640,128]{1,0:T(8,128)S(1)}, f32[640,128]{1,0:T(8,128)}, u32[]{:S(2)}) %copy-start.2) | copy-done | bytes 327704
  15.1 0.0 copy-start.4
  15.1 1.0 %copy-done.4 = f32[640,128]{1,0:T(8,128)S(1)} copy-done((f32[640,128]{1,0:T(8,128)S(1)}, f32[640,128]{1,0:T(8,128)}, u32[]{:S(2)}) %copy-start.4) | copy-done | bytes 327704
  16.1 0.0 copy-start.5
  16.1 0.8 %copy-done.5 = f32[128,128]{1,0:T(8,128)S(1)} copy-done((f32[128,128]{1,0:T(8,128)S(1)}, f32[128,128]{1,0:T(8,128)}, u32[]{:S(2)}) %copy-start.5) | copy-done | bytes 65560
  16.9 0.0 copy-start.7
  16.9 0.8 %copy-done.7 = f32[128,128]{1,0:T(8,128)S(1)} copy-done((f32[128,128]{1,0:T(8,128)S(1)}, f32[128,128]{1,0:T(8,128)}, u32[]{:S(2)}) %copy-start.7) | copy-done | bytes 65560
  17.8 5.0 %own_scores.1 = (f32[768,2048]{1,0:T(8,128)S(1)}, f32[768,2048]{1,0:T(8,128)S(1)}, f32[8,2048]{1,0:T(8,128)S(1)}) custom-call(s32[1]{0:T(128)S(6)} %copy.12.length_ref, f32[128,2048]{1,0:T(8,128)S(1)} %copy-done, f32[128,2048]{1,0:T(8,128)S(1)} %copy-done.1, f32[640,128]{1,0:T(8,128)S(1)} %copy-done.2, f32[128,128]{1,0:T(8,128)S(1)} %copy-done.5, ...), custom_call_target="tpu_custom_call" | custom-call | flops 3221225472 | bytes 12582912 | tf_op jit(solution)/shard_map/own_scores/pallas_call | solution.py:251
  22.8 0.0 collective-permute-done.refs_0_
  22.8 0.0 collective-permute-done.1.refs_1_
  22.9 1.3 %collective-permute-start.4 = (f32[320,128]{1,0:T(8,128)S(1)}, f32[320,128]{1,0:T(8,128)S(1)}, u32[]{:S(2)}, u32[]{:S(2)}) collective-permute-start(f32[320,128]{1,0:T(8,128)S(1)} %get-tuple-element.121), channel_id=1, source_target_pairs={{0,4},{4,0},{8,12},{12,8},{16,20},{20,16},{24,28},{28,24},{32,36},... | collective-permute-start | bytes 491528 | tf_op jit(solution)/shard_map/ppermute | solution.py:365
  24.2 2.4 %collective-permute-start.2 = (f32[320,128]{1,0:T(8,128)S(1)}, f32[320,128]{1,0:T(8,128)S(1)}, u32[]{:S(2)}, u32[]{:S(2)}) collective-permute-start(f32[320,128]{1,0:T(8,128)S(1)} %get-tuple-element.122), channel_id=1, source_target_pairs={{8,0},{12,4},{16,8},{20,12},{24,16},{28,20},{32,24},{36,28},{40,32... | collective-permute-start | bytes 491528 | tf_op jit(solution)/shard_map/ppermute | solution.py:359
  26.6 0.3 collective-permute-start.3
  26.9 1.9 %collective-permute-done.2.refs_2_ = f32[320,128]{1,0:T(8,128)S(1)} collective-permute-done((f32[320,128]{1,0:T(8,128)S(1)}, f32[320,128]{1,0:T(8,128)S(1)}, u32[]{:S(2)}, u32[]{:S(2)}) %collective-permute-start.2) | collective-permute-done | bytes 163872 | tf_op jit(solution)/shard_map/ppermute | solution.py:359
  28.8 0.5 collective-permute-start.5
  29.3 4.2 %far_scores.1 = (f32[640,2048]{1,0:T(8,128)S(1)}, f32[640,2048]{1,0:T(8,128)S(1)}, f32[8,2048]{1,0:T(8,128)S(1)}) custom-call(s32[1]{0:T(128)S(6)} %copy.12.length_ref, f32[128,2048]{1,0:T(8,128)S(1)} %copy-done, f32[128,2048]{1,0:T(8,128)S(1)} %copy-done.1, f32[640,128]{1,0:T(8,128)S(1)} %collective-permute-done.refs_0_, ...), custom_call_target="tpu_custom_call" | custom-call | flops 2684354560 | bytes 10485760 | tf_op jit(solution)/shard_map/far_scores/pallas_call | solution.py:251
  33.5 0.0 collective-permute-done.4.refs_0_
  33.5 3.7 %collective-permute-done.5.refs_1_ = f32[320,128]{1,0:T(8,128)S(1)} collective-permute-done((f32[320,128]{1,0:T(8,128)S(1)}, f32[320,128]{1,0:T(8,128)S(1)}, u32[]{:S(2)}, u32[]{:S(2)}) %collective-permute-start.5) | collective-permute-done | bytes 163872 | tf_op jit(solution)/shard_map/ppermute | solution.py:365
  37.2 0.0 collective-permute-done.3.k_ref
  37.3 7.3 %middle_pass.1 = (f32[128,2048]{1,0:T(8,128)S(1)}, f32[8,2048]{1,0:T(8,128)S(1)}, f32[640,128]{1,0:T(8,128)S(1)}, f32[640,128]{1,0:T(8,128)S(1)}) custom-call(s32[1]{0:T(128)S(6)} %copy.12.length_ref, f32[128,2048]{1,0:T(8,128)S(1)} %copy-done, f32[128,2048]{1,0:T(8,128)S(1)} %copy-done.1, f32[8,2048]{1,0:T(8,128)S(1)} %get-tuple-element.69.stats_a, ...), custom_call_target="tpu_custom_call" | custom-call | flops 6710886400 | bytes 5000000 | tf_op jit(solution)/shard_map/middle_pass/pallas_call | solution.py:268
  44.6 1.9 %collective-permute-start.6 = (f32[640,128]{1,0:T(8,128)S(1)}, f32[640,128]{1,0:T(8,128)S(1)}, u32[]{:S(2)}, u32[]{:S(2)}) collective-permute-start(f32[640,128]{1,0:T(8,128)S(1)} %get-tuple-element.79), channel_id=1, source_target_pairs={{0,4},{4,0},{8,12},{12,8},{16,20},{20,16},{24,28},{28,24},{32,36},... | collective-permute-start | bytes 983048 | tf_op jit(solution)/shard_map/ppermute | solution.py:365
  46.5 0.3 collective-permute-start.10
  46.8 0.0 copy-start.3
  46.8 0.0 copy-start.6
  46.8 5.8 %far_grads.1 = (f32[128,2048]{1,0:T(8,128)S(1)}, f32[640,128]{1,0:T(8,128)S(1)}, f32[640,128]{1,0:T(8,128)S(1)}) custom-call(s32[1]{0:T(128)S(6)} %copy.12.length_ref, s32[1]{0:T(128)} %bitcast.place_ref, f32[128,2048]{1,0:T(8,128)S(1)} %copy-done, f32[128,2048]{1,0:T(8,128)S(1)} %copy-done.1, f32[128,2048]{1,0:T(8,128)S(1)} %get-tuple-element.73.before_ref, ...), custom_call_target="tpu_custom_call" | custom-call | flops 4026531840 | bytes 10485760 | tf_op jit(solution)/shard_map/far_grads/pallas_call | solution.py:292
  52.6 0.0 collective-permute-done.6.near_ref
  52.7 1.2 %collective-permute-start.15 = (f32[640,128]{1,0:T(8,128)S(1)}, f32[640,128]{1,0:T(8,128)S(1)}, u32[]{:S(2)}, u32[]{:S(2)}) collective-permute-start(f32[640,128]{1,0:T(8,128)S(1)} %select_add_fusion.1), channel_id=1, source_target_pairs={{0,8},{4,12},{8,16},{12,20},{16,24},{20,28},{24,32},{28,36},{32,40... | collective-permute-start | bytes 983048 | tf_op jit(solution)/shard_map/ppermute | solution.py:362
  53.9 0.0 copy-done.3
  53.9 0.0 copy-done.6
  53.9 2.6 %own_grads_a.1 = (f32[32,1024]{1,0:T(8,128)S(1)}, f32[32,1024]{1,0:T(8,128)S(1)}, f32[32,1024]{1,0:T(8,128)S(1)}, f32[32,1024]{1,0:T(8,128)S(1)}, f32[640,128]{1...) custom-call(s32[1]{0:T(128)S(6)} %copy.12.length_ref, s32[1]{0:T(128)} %bitcast.place_ref, ...), custom_call_target="tpu_custom_call" | custom-call | flops 2415919104 | bytes 6291456 | tf_op jit(solution)/shard_map/own_grads_a/pallas_call | solution.py:292
  56.5 2.1 %collective-permute-done.10.near_ref = f32[640,128]{1,0:T(8,128)S(1)} collective-permute-done((f32[640,128]{1,0:T(8,128)S(1)}, f32[640,128]{1,0:T(8,128)S(1)}, u32[]{:S(2)}, u32[]{:S(2)}) %collective-permute-start.10) | collective-permute-done | bytes 327712 | tf_op jit(solution)/shard_map/ppermute | solution.py:365
  58.6 3.7 %collective-permute-start.7 = (f32[32,1024]{1,0:T(8,128)S(1)}, f32[32,1024]{1,0:T(8,128)S(1)}, u32[]{:S(2)}, u32[]{:S(2)}) collective-permute-start(f32[32,1024]{1,0:T(8,128)S(1)} %get-tuple-element.84), channel_id=1, source_target_pairs={{0,1},{1,0},{2,3},{3,2},{4,5},{5,4},{6,7},{7,6},{8,9},{9,8},{10,11... | collective-permute-start | bytes 393224 | tf_op jit(solution)/shard_map/ppermute | solution.py:368
  62.3 2.8 %collective-permute-start.8 = (f32[32,1024]{1,0:T(8,128)S(1)}, f32[32,1024]{1,0:T(8,128)S(1)}, u32[]{:S(2)}, u32[]{:S(2)}) collective-permute-start(f32[32,1024]{1,0:T(8,128)S(1)} %get-tuple-element.85), channel_id=1, source_target_pairs={{0,2},{1,3},{2,0},{3,1},{4,6},{5,7},{6,4},{7,5},{8,10},{9,11},{10,... | collective-permute-start | bytes 393224 | tf_op jit(solution)/shard_map/ppermute | solution.py:368
  65.1 0.5 collective-permute-start.9
  65.5 1.4 %collective-permute-start.14 = (f32[640,128]{1,0:T(8,128)S(1)}, f32[640,128]{1,0:T(8,128)S(1)}, u32[]{:S(2)}, u32[]{:S(2)}) collective-permute-start(f32[640,128]{1,0:T(8,128)S(1)} %select_add_fusion), channel_id=1, source_target_pairs={{0,8},{4,12},{8,16},{12,20},{16,24},{20,28},{24,32},{28,36},{32,40... | collective-permute-start | bytes 983048 | tf_op jit(solution)/shard_map/ppermute | solution.py:362
  66.9 2.6 %own_grads_b.1 = (f32[32,1024]{1,0:T(8,128)S(1)}, f32[32,1024]{1,0:T(8,128)S(1)}, f32[32,1024]{1,0:T(8,128)S(1)}, f32[32,1024]{1,0:T(8,128)S(1)}, f32[640,128]{1...) custom-call(s32[1]{0:T(128)S(6)} %copy.12.length_ref, s32[1]{0:T(128)} %bitcast.place_ref, ...), custom_call_target="tpu_custom_call" | custom-call | flops 2415919104 | bytes 6291456 | tf_op jit(solution)/shard_map/own_grads_b/pallas_call | solution.py:292
  69.5 0.0 collective-permute-done.7.refs_2_
  69.5 0.0 collective-permute-done.8.refs_4_
  69.5 2.8 %collective-permute-done.9.refs_6_ = f32[32,1024]{1,0:T(8,128)S(1)} collective-permute-done((f32[32,1024]{1,0:T(8,128)S(1)}, f32[32,1024]{1,0:T(8,128)S(1)}, u32[]{:S(2)}, u32[]{:S(2)}) %collective-permute-start.9) | collective-permute-done | bytes 131104 | tf_op jit(solution)/shard_map/ppermute | solution.py:368
  72.3 0.1 collective-permute-start.11
  72.4 2.4 %collective-permute-start.12 = (f32[32,1024]{1,0:T(8,128)S(1)}, f32[32,1024]{1,0:T(8,128)S(1)}, u32[]{:S(2)}, u32[]{:S(2)}) collective-permute-start(f32[32,1024]{1,0:T(8,128)S(1)} %get-tuple-element.105), channel_id=1, source_target_pairs={{0,2},{1,3},{2,0},{3,1},{4,6},{5,7},{6,4},{7,5},{8,10},{9,11},{10,... | collective-permute-start | bytes 393224 | tf_op jit(solution)/shard_map/ppermute | solution.py:368
  74.8 1.2 %collective-permute-start.13 = (f32[32,1024]{1,0:T(8,128)S(1)}, f32[32,1024]{1,0:T(8,128)S(1)}, u32[]{:S(2)}, u32[]{:S(2)}) collective-permute-start(f32[32,1024]{1,0:T(8,128)S(1)} %get-tuple-element.106), channel_id=1, source_target_pairs={{0,3},{1,2},{2,1},{3,0},{4,7},{5,6},{6,5},{7,4},{8,11},{9,10},{10,... | collective-permute-start | bytes 393224 | tf_op jit(solution)/shard_map/ppermute | solution.py:368
  76.0 0.0 collective-permute-done.15.far_ref
  76.0 0.8 sum_values.1
  76.8 1.3 %collective-permute-done.14.far_ref = f32[640,128]{1,0:T(8,128)S(1)} collective-permute-done((f32[640,128]{1,0:T(8,128)S(1)}, f32[640,128]{1,0:T(8,128)S(1)}, u32[]{:S(2)}, u32[]{:S(2)}) %collective-permute-start.14) | collective-permute-done | bytes 327712 | tf_op jit(solution)/shard_map/ppermute | solution.py:362
  78.0 0.8 sum_keys.1
  78.8 0.0 collective-permute-done.11.refs_3_
  78.8 0.0 collective-permute-done.12.refs_5_
  78.8 3.4 %collective-permute-done.13.refs_7_ = f32[32,1024]{1,0:T(8,128)S(1)} collective-permute-done((f32[32,1024]{1,0:T(8,128)S(1)}, f32[32,1024]{1,0:T(8,128)S(1)}, u32[]{:S(2)}, u32[]{:S(2)}) %collective-permute-start.13) | collective-permute-done | bytes 131104 | tf_op jit(solution)/shard_map/ppermute | solution.py:368
  82.2 1.0 %gather_queries.1 = f32[32,8192]{1,0:T(8,128)} custom-call(s32[1]{0:T(128)} %bitcast.place_ref, f32[32,1024]{1,0:T(8,128)S(1)} %get-tuple-element.102.refs_0_, f32[32,1024]{1,0:T(8,128)S(1)} %get-tuple-element.110.refs_1_, f32[32,1024]{1,0:T(8,128)S(1)} %collective-permute-done.7.refs_2_, f32[32,1024]{1,0:T(8,128)S(1)} %collective-permute-done.11.refs_3_, ...), custom_call_target="tpu_custom_call" | custom-call | tf_op jit(solution)/shard_map/gather_queries/pallas_call | solution.py:335
  (5 shorter events, 0.2 us)
Async XLA Ops:
  0.6 22.2 %collective-permute-start = (f32[640,128]{1,0:T(8,128)}, f32[640,128]{1,0:T(8,128)S(1)}, u32[]{:S(2)}, u32[]{:S(2)}) collective-permute-start(f32[640,128]{1,0:T(8,128)} %refs_0_.5), channel_id=1, source_target_pairs={{8,0},{12,4},{16,8},{20,12},{24,16},{28,20},{32,24},{36,28},{40,32... | collective-permute-start | bytes 983048 | tf_op jit(solution)/shard_map/ppermute | solution.py:359
  10.5 12.3 %collective-permute-start.1 = (f32[320,128]{1,0:T(8,128)S(1)}, f32[320,128]{1,0:T(8,128)S(1)}, u32[]{:S(2)}, u32[]{:S(2)}) collective-permute-start(f32[320,128]{1,0:T(8,128)S(1)} %slice.6), channel_id=1, source_target_pairs={{8,0},{12,4},{16,8},{20,12},{24,16},{28,20},{32,24},{36,28},{40,32... | collective-permute-start | bytes 491528 | tf_op jit(solution)/shard_map/ppermute | solution.py:359
  11.7 1.2 %copy-start = (f32[128,2048]{1,0:T(8,128)S(1)}, f32[128,2048]{1,0:T(8,128)}, u32[]{:S(2)}) copy-start(f32[128,2048]{1,0:T(8,128)} %q_ref.11) | copy-start | bytes 3145732
  12.9 1.2 %copy-start.1 = (f32[128,2048]{1,0:T(8,128)S(1)}, f32[128,2048]{1,0:T(8,128)}, u32[]{:S(2)}) copy-start(f32[128,2048]{1,0:T(8,128)} %g_ref.11) | copy-start | bytes 3145732
  14.1 1.0 %copy-start.2 = (f32[640,128]{1,0:T(8,128)S(1)}, f32[640,128]{1,0:T(8,128)}, u32[]{:S(2)}) copy-start(f32[640,128]{1,0:T(8,128)} %refs_0_.5) | copy-start | bytes 983044
  15.1 1.0 %copy-start.4 = (f32[640,128]{1,0:T(8,128)S(1)}, f32[640,128]{1,0:T(8,128)}, u32[]{:S(2)}) copy-start(f32[640,128]{1,0:T(8,128)} %refs_2_.1) | copy-start | bytes 983044
  16.1 0.8 %copy-start.5 = (f32[128,128]{1,0:T(8,128)S(1)}, f32[128,128]{1,0:T(8,128)}, u32[]{:S(2)}) copy-start(f32[128,128]{1,0:T(8,128)} %refs_1_.5) | copy-start | bytes 196612
  16.9 0.8 %copy-start.7 = (f32[128,128]{1,0:T(8,128)S(1)}, f32[128,128]{1,0:T(8,128)}, u32[]{:S(2)}) copy-start(f32[128,128]{1,0:T(8,128)} %refs_3_.1) | copy-start | bytes 196612
  22.9 10.7 %collective-permute-start.4 = (f32[320,128]{1,0:T(8,128)S(1)}, f32[320,128]{1,0:T(8,128)S(1)}, u32[]{:S(2)}, u32[]{:S(2)}) collective-permute-start(f32[320,128]{1,0:T(8,128)S(1)} %get-tuple-element.121), channel_id=1, source_target_pairs={{0,4},{4,0},{8,12},{12,8},{16,20},{20,16},{24,28},{28,24},{32,36},... | collective-permute-start | bytes 491528 | tf_op jit(solution)/shard_map/ppermute | solution.py:365
  24.2 4.6 %collective-permute-start.2 = (f32[320,128]{1,0:T(8,128)S(1)}, f32[320,128]{1,0:T(8,128)S(1)}, u32[]{:S(2)}, u32[]{:S(2)}) collective-permute-start(f32[320,128]{1,0:T(8,128)S(1)} %get-tuple-element.122), channel_id=1, source_target_pairs={{8,0},{12,4},{16,8},{20,12},{24,16},{28,20},{32,24},{36,28},{40,32... | collective-permute-start | bytes 491528 | tf_op jit(solution)/shard_map/ppermute | solution.py:359
  26.6 10.7 %collective-permute-start.3 = (f32[640,128]{1,0:T(8,128)S(1)}, f32[640,128]{1,0:T(8,128)S(1)}, u32[]{:S(2)}, u32[]{:S(2)}) collective-permute-start(f32[640,128]{1,0:T(8,128)S(1)} %broadcast_select_fusion), channel_id=1, source_target_pairs={{0,4},{4,0},{8,12},{12,8},{16,20},{20,16},{24,28},{28,24},{32,36},... | collective-permute-start | bytes 983048 | tf_op jit(solution)/shard_map/ppermute | solution.py:365
  28.8 8.4 %collective-permute-start.5 = (f32[320,128]{1,0:T(8,128)S(1)}, f32[320,128]{1,0:T(8,128)S(1)}, u32[]{:S(2)}, u32[]{:S(2)}) collective-permute-start(f32[320,128]{1,0:T(8,128)S(1)} %broadcast_select_fusion.2), channel_id=1, source_target_pairs={{0,4},{4,0},{8,12},{12,8},{16,20},{20,16},{24,28},{28,24},{32,36},... | collective-permute-start | bytes 491528 | tf_op jit(solution)/shard_map/ppermute | solution.py:365
  44.6 8.1 %collective-permute-start.6 = (f32[640,128]{1,0:T(8,128)S(1)}, f32[640,128]{1,0:T(8,128)S(1)}, u32[]{:S(2)}, u32[]{:S(2)}) collective-permute-start(f32[640,128]{1,0:T(8,128)S(1)} %get-tuple-element.79), channel_id=1, source_target_pairs={{0,4},{4,0},{8,12},{12,8},{16,20},{20,16},{24,28},{28,24},{32,36},... | collective-permute-start | bytes 983048 | tf_op jit(solution)/shard_map/ppermute | solution.py:365
  46.5 12.1 %collective-permute-start.10 = (f32[640,128]{1,0:T(8,128)S(1)}, f32[640,128]{1,0:T(8,128)S(1)}, u32[]{:S(2)}, u32[]{:S(2)}) collective-permute-start(f32[640,128]{1,0:T(8,128)S(1)} %get-tuple-element.92), channel_id=1, source_target_pairs={{0,4},{4,0},{8,12},{12,8},{16,20},{20,16},{24,28},{28,24},{32,36},... | collective-permute-start | bytes 983048 | tf_op jit(solution)/shard_map/ppermute | solution.py:365
  46.8 7.1 %copy-start.3 = (f32[640,128]{1,0:T(8,128)S(1)}, f32[640,128]{1,0:T(8,128)}, u32[]{:S(2)}) copy-start(f32[640,128]{1,0:T(8,128)} %refs_0_.5) | copy-start | bytes 983044
  46.8 7.1 %copy-start.6 = (f32[128,128]{1,0:T(8,128)S(1)}, f32[128,128]{1,0:T(8,128)}, u32[]{:S(2)}) copy-start(f32[128,128]{1,0:T(8,128)} %refs_1_.5) | copy-start | bytes 196612
  52.7 23.3 %collective-permute-start.15 = (f32[640,128]{1,0:T(8,128)S(1)}, f32[640,128]{1,0:T(8,128)S(1)}, u32[]{:S(2)}, u32[]{:S(2)}) collective-permute-start(f32[640,128]{1,0:T(8,128)S(1)} %select_add_fusion.1), channel_id=1, source_target_pairs={{0,8},{4,12},{8,16},{12,20},{16,24},{20,28},{24,32},{28,36},{32,40... | collective-permute-start | bytes 983048 | tf_op jit(solution)/shard_map/ppermute | solution.py:362
  58.6 10.9 %collective-permute-start.7 = (f32[32,1024]{1,0:T(8,128)S(1)}, f32[32,1024]{1,0:T(8,128)S(1)}, u32[]{:S(2)}, u32[]{:S(2)}) collective-permute-start(f32[32,1024]{1,0:T(8,128)S(1)} %get-tuple-element.84), channel_id=1, source_target_pairs={{0,1},{1,0},{2,3},{3,2},{4,5},{5,4},{6,7},{7,6},{8,9},{9,8},{10,11... | collective-permute-start | bytes 393224 | tf_op jit(solution)/shard_map/ppermute | solution.py:368
  62.3 7.2 %collective-permute-start.8 = (f32[32,1024]{1,0:T(8,128)S(1)}, f32[32,1024]{1,0:T(8,128)S(1)}, u32[]{:S(2)}, u32[]{:S(2)}) collective-permute-start(f32[32,1024]{1,0:T(8,128)S(1)} %get-tuple-element.85), channel_id=1, source_target_pairs={{0,2},{1,3},{2,0},{3,1},{4,6},{5,7},{6,4},{7,5},{8,10},{9,11},{10,... | collective-permute-start | bytes 393224 | tf_op jit(solution)/shard_map/ppermute | solution.py:368
  65.1 7.3 %collective-permute-start.9 = (f32[32,1024]{1,0:T(8,128)S(1)}, f32[32,1024]{1,0:T(8,128)S(1)}, u32[]{:S(2)}, u32[]{:S(2)}) collective-permute-start(f32[32,1024]{1,0:T(8,128)S(1)} %get-tuple-element.86), channel_id=1, source_target_pairs={{0,3},{1,2},{2,1},{3,0},{4,7},{5,6},{6,5},{7,4},{8,11},{9,10},{10,... | collective-permute-start | bytes 393224 | tf_op jit(solution)/shard_map/ppermute | solution.py:368
  65.5 12.5 %collective-permute-start.14 = (f32[640,128]{1,0:T(8,128)S(1)}, f32[640,128]{1,0:T(8,128)S(1)}, u32[]{:S(2)}, u32[]{:S(2)}) collective-permute-start(f32[640,128]{1,0:T(8,128)S(1)} %select_add_fusion), channel_id=1, source_target_pairs={{0,8},{4,12},{8,16},{12,20},{16,24},{20,28},{24,32},{28,36},{32,40... | collective-permute-start | bytes 983048 | tf_op jit(solution)/shard_map/ppermute | solution.py:362
  72.3 6.5 %collective-permute-start.11 = (f32[32,1024]{1,0:T(8,128)S(1)}, f32[32,1024]{1,0:T(8,128)S(1)}, u32[]{:S(2)}, u32[]{:S(2)}) collective-permute-start(f32[32,1024]{1,0:T(8,128)S(1)} %get-tuple-element.104), channel_id=1, source_target_pairs={{0,1},{1,0},{2,3},{3,2},{4,5},{5,4},{6,7},{7,6},{8,9},{9,8},{10,11... | collective-permute-start | bytes 393224 | tf_op jit(solution)/shard_map/ppermute | solution.py:368
  72.4 6.4 %collective-permute-start.12 = (f32[32,1024]{1,0:T(8,128)S(1)}, f32[32,1024]{1,0:T(8,128)S(1)}, u32[]{:S(2)}, u32[]{:S(2)}) collective-permute-start(f32[32,1024]{1,0:T(8,128)S(1)} %get-tuple-element.105), channel_id=1, source_target_pairs={{0,2},{1,3},{2,0},{3,1},{4,6},{5,7},{6,4},{7,5},{8,10},{9,11},{10,... | collective-permute-start | bytes 393224 | tf_op jit(solution)/shard_map/ppermute | solution.py:368
  74.8 7.4 %collective-permute-start.13 = (f32[32,1024]{1,0:T(8,128)S(1)}, f32[32,1024]{1,0:T(8,128)S(1)}, u32[]{:S(2)}, u32[]{:S(2)}) collective-permute-start(f32[32,1024]{1,0:T(8,128)S(1)} %get-tuple-element.106), channel_id=1, source_target_pairs={{0,3},{1,2},{2,1},{3,0},{4,7},{5,6},{6,5},{7,4},{8,11},{9,10},{10,... | collective-permute-start | bytes 393224 | tf_op jit(solution)/shard_map/ppermute | solution.py:368
